TPU v7x, 256 devices: a whole 4x4x8 slice. The times are simulated.
256 devices in a mesh: dp: 8 (over z), ctx: 8 (over x, core), exp: 4 (over y).
Axes of the slice: x: 4, y: 4, z: 8, core: 2. Of those that a mesh axis runs over, the one named last changes fastest.
Arguments:
- queries: bfloat16 [32768, 4096], P(('dp', 'ctx', 'exp')), parts along dimension 0, may hold values from -6 to 6
- key_rows: bfloat16 [32768, 4096], P(('dp', 'ctx', 'exp')), parts along dimension 0, may hold values from -6 to 6
- value_rows: bfloat16 [32768, 4096], P(('dp', 'ctx', 'exp')), parts along dimension 0, may hold values from -6 to 6
- residual: bfloat16 [32768, 4096], P(('dp', 'ctx', 'exp')), parts along dimension 0, may hold values from -18 to 18
- lambdas: float32 [32], replicated, may hold values from 0.2 to 0.8
- router: bfloat16 [4096, 8], replicated, may hold values from -0.09375 to 0.09375
- gate_proj: bfloat16 [8, 4096, 1024], P('ctx', None, 'exp'), may hold values from -0.09375 to 0.09375
- up_proj: bfloat16 [8, 4096, 1024], P('ctx', None, 'exp'), may hold values from -0.09375 to 0.09375
- down_proj: bfloat16 [8, 4096, 1024], P('ctx', None, 'exp'), may hold values from -0.1875 to 0.1875
- routes: int32 [32768, 2], P(('dp', 'ctx', 'exp')), parts along dimension 0, may hold values from 0 to 7, as said below
- capacity: int32 [256, 8], P(('dp', 'ctx', 'exp')), parts along dimension 0, may hold values from 18 to 36, as said below
Outputs:
- layer_out: bfloat16 [32768, 4096], P(('dp', 'ctx', 'exp')), parts along dimension 0
There are 8 independent parts, one for each index of `dp`. A program takes and returns all parts, laid end to end along the dimension named above; an argument that names none is the same for every part. Nothing has to cross between parts.
Inputs may be any that keep to these rules, and one draw needn't show every extreme that they name: `routes`: each row names two different experts. For one expert H, drawn from the seed, at least 36 tokens of every block of 128 tokens name it. capacity[b, H] = 36 for every block b, H being the expert of the routes' promise.
All inputs are finite; a program needn't handle non-finite values.
Results may differ from a plain program's by a relative error of at most 0.0042.
Values may be sent and summed in bfloat16 or wider, within the bound.
A program may use at most 128 MiB of HBM per device.

v0:
```python
from functools import partial
import math

import jax
import jax.numpy as jnp
from jax import lax
from jax.sharding import PartitionSpec as P

HEADS = 32


epsilon = 1e-05
out_scale = 0.8
contract_last = (((1,), (1,)), ((), ()))


def head_block(q_pair, k_pair, v_head, weight_two, block_len, block_index):
    map_width = q_pair.shape[1] // 2
    score_scale = 1.0 / math.sqrt(map_width)
    row_start = block_index * block_len
    q_block = lax.dynamic_slice_in_dim(q_pair, row_start, block_len, 0)
    row_pos = row_start + jnp.arange(block_len)

    def block_scores(key_index):
        col_start = key_index * block_len
        k_block = lax.dynamic_slice_in_dim(k_pair, col_start, block_len, 0)
        allowed = (col_start + jnp.arange(block_len))[None, :] <= row_pos[:, None]
        both_maps = []
        for map_index in range(2):
            first_col = map_index * map_width
            scores = (
                lax.dot_general(
                    q_block[:, first_col : first_col + map_width],
                    k_block[:, first_col : first_col + map_width],
                    contract_last,
                    preferred_element_type=jnp.float32,
                )
                * score_scale
            )
            both_maps.append(jnp.where(allowed, scores, -jnp.inf))
        return both_maps

    def gather_stats(key_index, carried):
        both_maps = block_scores(key_index)
        updated = []
        for map_index in range(2):
            largest, totals = carried[map_index]
            new_largest = jnp.maximum(largest, jnp.max(both_maps[map_index], axis=1))
            totals = totals * jnp.exp(largest - new_largest) + jnp.sum(
                jnp.exp(both_maps[map_index] - new_largest[:, None]), axis=1
            )
            updated.append((new_largest, totals))
        return tuple(updated)

    start_stats = tuple(
        (
            (jnp.full((block_len,), -jnp.inf, jnp.float32), jnp.zeros((block_len,), jnp.float32))
            for map_index in range(2)
        )
    )
    stats = lax.fori_loop(0, block_index + 1, gather_stats, start_stats)

    def accumulate(key_index, mixed_rows):
        both_maps = block_scores(key_index)
        probs_one = jnp.exp(both_maps[0] - stats[0][0][:, None]) / stats[0][1][:, None]
        probs_two = jnp.exp(both_maps[1] - stats[1][0][:, None]) / stats[1][1][:, None]
        weights = (probs_one - weight_two * probs_two).astype(jnp.bfloat16)
        v_block = lax.dynamic_slice_in_dim(v_head, key_index * block_len, block_len, 0)
        return mixed_rows + jnp.dot(weights, v_block, preferred_element_type=jnp.float32)

    mixed_rows = lax.fori_loop(
        0, block_index + 1, accumulate, jnp.zeros((block_len, v_head.shape[1]), jnp.float32)
    )
    normed = (
        out_scale
        * mixed_rows
        * lax.rsqrt(jnp.mean(mixed_rows * mixed_rows, axis=1, keepdims=True) + epsilon)
    )
    return normed.astype(jnp.bfloat16)


def head_attention(q_pair, k_pair, v_head, weight_two):
    length = q_pair.shape[0]
    block_len = 512
    blocks = lax.map(
        partial(head_block, q_pair, k_pair, v_head, weight_two, block_len),
        jnp.arange(length // block_len),
    )
    return blocks.reshape(length, v_head.shape[1])


def expert_part(token_rows, gate_w, up_w, down_w):
    gate_out = jnp.dot(token_rows, gate_w, preferred_element_type=jnp.float32)
    up_out = jnp.dot(token_rows, up_w, preferred_element_type=jnp.float32)
    hidden = (jax.nn.silu(gate_out) * up_out).astype(jnp.bfloat16)
    return lax.dot_general(
        hidden, down_w, contract_last, preferred_element_type=jnp.float32
    ).astype(jnp.bfloat16)


def shards(
    queries,
    key_rows,
    value_rows,
    residual,
    lambdas,
    router,
    gate_proj,
    up_proj,
    down_proj,
    routes,
    capacity,
):
    tokens_here, width = queries.shape
    query_heads, key_heads, value_heads = (
        lax.all_to_all(queries, ("ctx", "exp"), split_axis=1, concat_axis=0, tiled=True),
        lax.all_to_all(key_rows, ("ctx", "exp"), split_axis=1, concat_axis=0, tiled=True),
        lax.all_to_all(value_rows, ("ctx", "exp"), split_axis=1, concat_axis=0, tiled=True),
    )
    span = width // HEADS
    heads_here = query_heads.shape[1] // span
    first_head = lax.axis_index(("ctx", "exp")) * heads_here
    weight_two = lax.dynamic_index_in_dim(lambdas, first_head + 0, keepdims=False)
    outputs = head_attention(query_heads, key_heads, value_heads, weight_two)
    returned = lax.all_to_all(outputs, ("ctx", "exp"), split_axis=0, concat_axis=1, tiled=True)
    attended = residual.astype(jnp.float32) + returned.astype(jnp.float32)
    normed = (
        attended * lax.rsqrt(jnp.mean(attended * attended, axis=1, keepdims=True) + epsilon)
    ).astype(jnp.bfloat16)
    experts = router.shape[1]
    logits = jnp.dot(normed, router, preferred_element_type=jnp.float32)
    chosen_mask = routes[:, :, None] == jnp.arange(experts, dtype=jnp.int32)[None, None, :]
    picked_sig = jnp.sum(jnp.where(chosen_mask, jax.nn.sigmoid(logits)[:, None, :], 0.0), axis=2)
    gates = picked_sig / jnp.sum(picked_sig, axis=1, keepdims=True)
    one_hot = chosen_mask.reshape(tokens_here * 2, experts).astype(jnp.int32)
    earlier = jnp.cumsum(one_hot, axis=0) - one_hot
    position = jnp.sum(earlier * one_hot, axis=1)
    allowance = jnp.sum(capacity[0][None, :] * one_hot, axis=1)
    kept = position < allowance
    slot_cap = min(9 * tokens_here // (4 * experts), tokens_here)
    full_slots = experts * slot_cap
    target = jnp.where(kept, routes.reshape(-1) * slot_cap + position, full_slots)
    buffer = (
        jnp.zeros((full_slots, width), jnp.bfloat16)
        .at[target]
        .set(jnp.repeat(normed, 2, axis=0), mode="drop")
    )
    buffer = buffer.reshape(experts, slot_cap, width)
    gate_w = gate_proj[0]
    up_w = up_proj[0]
    down_w = down_proj[0]
    fan_out = lax.axis_size("exp")
    outgoing = jnp.broadcast_to(buffer[:, None], (experts, fan_out, slot_cap, width))
    outgoing = outgoing.reshape(experts * fan_out, slot_cap, width)
    arrived = lax.all_to_all(outgoing, ("ctx", "exp"), split_axis=0, concat_axis=0, tiled=True)
    item_count = arrived.shape[1]
    parts_made = expert_part(arrived.reshape(-1, width), gate_w, up_w, down_w)
    parts_made = parts_made.reshape(arrived.shape[0], item_count, width)
    home = lax.all_to_all(parts_made, ("ctx", "exp"), split_axis=0, concat_axis=0, tiled=True)
    summed = jnp.sum(home.reshape(experts, fan_out, item_count, width).astype(jnp.float32), axis=1)
    results = summed.astype(jnp.bfloat16)
    results = results.reshape(full_slots, width)
    picked = jnp.take(results, jnp.minimum(target, full_slots - 1), axis=0)
    share = jnp.where(kept, gates.reshape(-1), 0.0)
    expert_sum = jnp.sum(
        (picked.astype(jnp.float32) * share[:, None]).reshape(tokens_here, 2, width), axis=1
    )
    return (attended + expert_sum).astype(jnp.bfloat16)


def solution(mesh):
    placed = (
        P(("dp", "ctx", "exp"), None),
        P(("dp", "ctx", "exp"), None),
        P(("dp", "ctx", "exp"), None),
        P(("dp", "ctx", "exp"), None),
        P(),
        P(),
        P("ctx", None, "exp"),
        P("ctx", None, "exp"),
        P("ctx", None, "exp"),
        P(("dp", "ctx", "exp"), None),
        P(("dp", "ctx", "exp"), None),
    )
    return jax.shard_map(
        shards, mesh=mesh, in_specs=placed, out_specs=P(("dp", "ctx", "exp"), None), check_vma=False
    )
```

profile of v0, /device:TPU:120, one launch (start us, length us, event | category | flops | bytes accessed | tf_op | source)
XLA Modules:
  0.0 823.8 jit_solution(9988714107336833698)
XLA Ops:
  12.5 12.9 %all-to-all-done = bf16[128,32,128]{2,0,1:T(8,128)(2,1)S(1)} async-done(((bf16[128,32,128]{2,0,1:T(8,128)(2,1)}), bf16[128,32,128]{2,0,1:T(8,128)(2,1)S(1)}, u32[]{:S(2)}, u32[]{:S(2)}) %all-to-all-start) | async-done | bytes 1048608 | tf_op jit(solution)/shard_map/all_to_all | solution.py:116
  34.1 13.0 %all-to-all-done.1 = bf16[128,32,128]{2,0,1:T(8,128)(2,1)} async-done(((bf16[128,32,128]{2,0,1:T(8,128)(2,1)}), bf16[128,32,128]{2,0,1:T(8,128)(2,1)}, u32[]{:S(2)}, u32[]{:S(2)}) %all-to-all-start.1) | async-done | bytes 1048608 | tf_op jit(solution)/shard_map/all_to_all | solution.py:117
  55.4 13.5 %all-to-all-done.2 = bf16[128,32,128]{2,0,1:T(8,128)(2,1)} async-done(((bf16[128,32,128]{2,0,1:T(8,128)(2,1)}), bf16[128,32,128]{2,0,1:T(8,128)(2,1)}, u32[]{:S(2)}, u32[]{:S(2)}) %all-to-all-start.2) | async-done | bytes 1048608 | tf_op jit(solution)/shard_map/all_to_all | solution.py:118
  69.5 340.4 %while.40 = (s32[]{:T(128)}, bf16[8,512,128]{2,1,0:T(8,128)(2,1)}, s32[8]{0:T(128)}, bf16[4096,128]{1,0:T(8,128)(2,1)S(1)}, bf16[4096,128]{1,0:T(8,128)(2,1)}, /...) while((s32[]{:T(128)}, bf16[8,512,128]{2,1,0:T(8,128)(2,1)}, ...), condition=%wide.region_10.11_spmd, body=%wide.region_0.10_spmd.sunk | while | flops 208212992 | bytes 9296441 | solution.py:85
  90.5 11.2 %while.42 = (s32[]{:T(128)}, f32[512,128]{1,0:T(8,128)S(1)}, s32[]{:T(128)}, bf16[4096,128]{1,0:T(8,128)(2,1)}, bf16[512,128]{1,0:T(8,128)(2,1)S(1)}, /*index=5*...) while((s32[]{:T(128)}, f32[512,128]{1,0:T(8,128)S(1)}, ...), condition=%wide.region_8.8_spmd.clone, body=%wide.region_7.7_spmd.clone.sunk | while | flops 137692160 | bytes 3315487 | solution.py:71
  105.3 9.1 %while.41 = (s32[]{:T(128)}, f32[512]{0:T(512)S(1)}, f32[512]{0:T(512)S(1)}, f32[512]{0:T(512)S(1)}, f32[512]{0:T(512)S(1)}, /*index=5*/s32[]{:T(128)}, bf16[409...) while((s32[]{:T(128)}, f32[512]{0:T(512)S(1)}, ...), condition=%wide.region_6.6_spmd.clone, body=%wide.region_1.5_spmd.clone.sunk | while | flops 70257664 | bytes 4784339 | solution.py:61
  114.4 16.8 %while.42 = (s32[]{:T(128)}, f32[512,128]{1,0:T(8,128)S(1)}, s32[]{:T(128)}, bf16[4096,128]{1,0:T(8,128)(2,1)}, bf16[512,128]{1,0:T(8,128)(2,1)S(1)}, /*index=5*...) while((s32[]{:T(128)}, f32[512,128]{1,0:T(8,128)S(1)}, ...), condition=%wide.region_8.8_spmd.clone, body=%wide.region_7.7_spmd.clone.sunk | while | flops 137692160 | bytes 3315487 | solution.py:71
  134.9 12.2 %while.41 = (s32[]{:T(128)}, f32[512]{0:T(512)S(1)}, f32[512]{0:T(512)S(1)}, f32[512]{0:T(512)S(1)}, f32[512]{0:T(512)S(1)}, /*index=5*/s32[]{:T(128)}, bf16[409...) while((s32[]{:T(128)}, f32[512]{0:T(512)S(1)}, ...), condition=%wide.region_6.6_spmd.clone, body=%wide.region_1.5_spmd.clone.sunk | while | flops 70257664 | bytes 4784339 | solution.py:61
  147.1 22.4 %while.42 = (s32[]{:T(128)}, f32[512,128]{1,0:T(8,128)S(1)}, s32[]{:T(128)}, bf16[4096,128]{1,0:T(8,128)(2,1)}, bf16[512,128]{1,0:T(8,128)(2,1)S(1)}, /*index=5*...) while((s32[]{:T(128)}, f32[512,128]{1,0:T(8,128)S(1)}, ...), condition=%wide.region_8.8_spmd.clone, body=%wide.region_7.7_spmd.clone.sunk | while | flops 137692160 | bytes 3315487 | solution.py:71
  173.1 15.2 %while.41 = (s32[]{:T(128)}, f32[512]{0:T(512)S(1)}, f32[512]{0:T(512)S(1)}, f32[512]{0:T(512)S(1)}, f32[512]{0:T(512)S(1)}, /*index=5*/s32[]{:T(128)}, bf16[409...) while((s32[]{:T(128)}, f32[512]{0:T(512)S(1)}, ...), condition=%wide.region_6.6_spmd.clone, body=%wide.region_1.5_spmd.clone.sunk | while | flops 70257664 | bytes 4784339 | solution.py:61
  188.3 28.1 %while.42 = (s32[]{:T(128)}, f32[512,128]{1,0:T(8,128)S(1)}, s32[]{:T(128)}, bf16[4096,128]{1,0:T(8,128)(2,1)}, bf16[512,128]{1,0:T(8,128)(2,1)S(1)}, /*index=5*...) while((s32[]{:T(128)}, f32[512,128]{1,0:T(8,128)S(1)}, ...), condition=%wide.region_8.8_spmd.clone, body=%wide.region_7.7_spmd.clone.sunk | while | flops 137692160 | bytes 3315487 | solution.py:71
  220.0 18.3 %while.41 = (s32[]{:T(128)}, f32[512]{0:T(512)S(1)}, f32[512]{0:T(512)S(1)}, f32[512]{0:T(512)S(1)}, f32[512]{0:T(512)S(1)}, /*index=5*/s32[]{:T(128)}, bf16[409...) while((s32[]{:T(128)}, f32[512]{0:T(512)S(1)}, ...), condition=%wide.region_6.6_spmd.clone, body=%wide.region_1.5_spmd.clone.sunk | while | flops 70257664 | bytes 4784339 | solution.py:61
  238.3 33.7 %while.42 = (s32[]{:T(128)}, f32[512,128]{1,0:T(8,128)S(1)}, s32[]{:T(128)}, bf16[4096,128]{1,0:T(8,128)(2,1)}, bf16[512,128]{1,0:T(8,128)(2,1)S(1)}, /*index=5*...) while((s32[]{:T(128)}, f32[512,128]{1,0:T(8,128)S(1)}, ...), condition=%wide.region_8.8_spmd.clone, body=%wide.region_7.7_spmd.clone.sunk | while | flops 137692160 | bytes 3315487 | solution.py:71
  275.5 21.3 %while.41 = (s32[]{:T(128)}, f32[512]{0:T(512)S(1)}, f32[512]{0:T(512)S(1)}, f32[512]{0:T(512)S(1)}, f32[512]{0:T(512)S(1)}, /*index=5*/s32[]{:T(128)}, bf16[409...) while((s32[]{:T(128)}, f32[512]{0:T(512)S(1)}, ...), condition=%wide.region_6.6_spmd.clone, body=%wide.region_1.5_spmd.clone.sunk | while | flops 70257664 | bytes 4784339 | solution.py:61
  296.8 39.3 %while.42 = (s32[]{:T(128)}, f32[512,128]{1,0:T(8,128)S(1)}, s32[]{:T(128)}, bf16[4096,128]{1,0:T(8,128)(2,1)}, bf16[512,128]{1,0:T(8,128)(2,1)S(1)}, /*index=5*...) while((s32[]{:T(128)}, f32[512,128]{1,0:T(8,128)S(1)}, ...), condition=%wide.region_8.8_spmd.clone, body=%wide.region_7.7_spmd.clone.sunk | while | flops 137692160 | bytes 3315487 | solution.py:71
  339.7 24.3 %while.41 = (s32[]{:T(128)}, f32[512]{0:T(512)S(1)}, f32[512]{0:T(512)S(1)}, f32[512]{0:T(512)S(1)}, f32[512]{0:T(512)S(1)}, /*index=5*/s32[]{:T(128)}, bf16[409...) while((s32[]{:T(128)}, f32[512]{0:T(512)S(1)}, ...), condition=%wide.region_6.6_spmd.clone, body=%wide.region_1.5_spmd.clone.sunk | while | flops 70257664 | bytes 4784339 | solution.py:61
  364.1 44.9 %while.42 = (s32[]{:T(128)}, f32[512,128]{1,0:T(8,128)S(1)}, s32[]{:T(128)}, bf16[4096,128]{1,0:T(8,128)(2,1)}, bf16[512,128]{1,0:T(8,128)(2,1)S(1)}, /*index=5*...) while((s32[]{:T(128)}, f32[512,128]{1,0:T(8,128)S(1)}, ...), condition=%wide.region_8.8_spmd.clone, body=%wide.region_7.7_spmd.clone.sunk | while | flops 137692160 | bytes 3315487 | solution.py:71
  418.0 14.1 %all-to-all-done.3 = bf16[32,128,128]{2,1,0:T(8,128)(2,1)} async-done(((bf16[32,128,128]{2,1,0:T(8,128)(2,1)}), bf16[32,128,128]{2,1,0:T(8,128)(2,1)}, u32[]{:S(2)}, u32[]{:S(2)}) %all-to-all-start.3) | async-done | bytes 1048608 | tf_op jit(solution)/shard_map/all_to_all | solution.py:125
  466.0 124.5 %all_to_all.80 = bf16[32,36,4096]{2,1,0:T(8,128)(2,1)} all-to-all(bf16[32,36,4096]{2,1,0:T(8,128)(2,1)} %bitcast.114), channel_id=1, replica_groups=mesh['dp'=8,'ctx'=8,'exp'=4] {'ctx','exp'}, dimensions={0} | all-to-all | bytes 18874368 | tf_op jit(solution)/shard_map/all_to_all | solution.py:155
  590.5 13.3 %reshape.195 = bf16[1152,4096]{1,0:T(8,128)(2,1)} reshape(bf16[32,36,4096]{2,1,0:T(8,128)(2,1)} %all_to_all.80) | data formatting | bytes 18874368 | tf_op jit(solution)/shard_map/reshape | solution.py:157
  619.3 13.1 %reshape.196 = bf16[32,36,4096]{2,1,0:T(8,128)(2,1)} reshape(bf16[1152,4096]{1,0:T(8,128)(2,1)} %convolution_convert_fusion) | data formatting | bytes 18874368 | tf_op jit(solution)/shard_map/reshape | solution.py:158
  640.4 146.7 %all-to-all-done.5 = bf16[32,36,4096]{2,1,0:T(8,128)(2,1)} async-done(((bf16[32,36,4096]{2,1,0:T(8,128)(2,1)}), bf16[32,36,4096]{2,1,0:T(8,128)(2,1)}, u32[]{:S(2)}, u32[]{:S(2)}) %all-to-all-start.5) | async-done | bytes 9437216 | tf_op jit(solution)/shard_map/all_to_all | solution.py:159
  787.0 8.4 %bitcast_reduce_fusion = bf16[8,36,4096]{2,1,0:T(8,128)(2,1)} fusion(bf16[32,36,4096]{2,1,0:T(8,128)(2,1)} %all-to-all-done.5), kind=kLoop, calls=%fused_computation.61 | loop fusion | flops 3538944 | bytes 11796480 | tf_op jit(solution)/shard_map/reduce_sum | solution.py:160
  811.3 10.9 %multiply_reduce_fusion.1 = f32[128,4096]{1,0:T(8,128)S(1)} fusion(bf16[128,2,4096]{2,1,0:T(2,128)(2,1)} %gather.7, pred[128,2]{1,0:T(8,128)(4,1)S(1)} %copy.69, f32[128,2]{1,0:T(8,128)S(1)} %copy.71), kind=kLoop, calls=%fused_computation.62 | loop fusion | flops 3670016 | bytes 4195584 | tf_op jit(solution)/shard_map/reduce_sum | solution.py:165
  (815 shorter events, 452.2 us)
Async XLA Ops:
  0.0 614.2 %copy-start = (bf16[1,4096,256]{2,1,0:T(8,128)(2,1)S(1)}, bf16[1,4096,256]{2,1,0:T(8,128)(2,1)}, u32[]{:S(2)}) copy-start(bf16[1,4096,256]{2,1,0:T(8,128)(2,1)} %param.25) | copy-start | bytes 6291460
  2.6 22.7 %all-to-all-start = ((bf16[128,32,128]{2,0,1:T(8,128)(2,1)}), bf16[128,32,128]{2,0,1:T(8,128)(2,1)S(1)}, u32[]{:S(2)}, u32[]{:S(2)}) async-start(bf16[128,32,128]{2,0,1:T(8,128)(2,1)} %copy_bitcast_fusion.2), calls=%async_computation | async-start | bytes 2097152 | tf_op jit(solution)/shard_map/all_to_all | solution.py:116
  25.4 21.8 %all-to-all-start.1 = ((bf16[128,32,128]{2,0,1:T(8,128)(2,1)}), bf16[128,32,128]{2,0,1:T(8,128)(2,1)}, u32[]{:S(2)}, u32[]{:S(2)}) async-start(bf16[128,32,128]{2,0,1:T(8,128)(2,1)} %copy_bitcast_fusion.1), calls=%async_computation.1 | async-start | bytes 2097152 | tf_op jit(solution)/shard_map/all_to_all | solution.py:117
  31.6 21.8 %copy-start.10 = (s32[128,2]{0,1:T(2,128)S(1)}, s32[128,2]{0,1:T(2,128)}, u32[]{:S(2)}) copy-start(s32[128,2]{0,1:T(2,128)} %param.26) | copy-start | bytes 3076
  31.6 23.3 %copy-start.16 = (f32[32]{0:T(128)S(1)}, f32[32]{0:T(128)}, u32[]{:S(2)}) copy-start(f32[32]{0:T(128)} %param.21) | copy-start | bytes 388
  47.1 21.8 %all-to-all-start.2 = ((bf16[128,32,128]{2,0,1:T(8,128)(2,1)}), bf16[128,32,128]{2,0,1:T(8,128)(2,1)}, u32[]{:S(2)}, u32[]{:S(2)}) async-start(bf16[128,32,128]{2,0,1:T(8,128)(2,1)} %copy_bitcast_fusion), calls=%async_computation.2 | async-start | bytes 2097152 | tf_op jit(solution)/shard_map/all_to_all | solution.py:118
  75.2 0.6 copy-start.7
  90.5 0.6 copy-start.7
  96.1 0.6 copy-start.7
  114.5 0.6 copy-start.7
  409.9 6.8 copy-start.11
  409.9 7.1 copy-start.13
  409.9 8.0 copy-start.12
  409.9 8.0 copy-start.14
  409.9 22.2 %all-to-all-start.3 = ((bf16[32,128,128]{2,1,0:T(8,128)(2,1)}), bf16[32,128,128]{2,1,0:T(8,128)(2,1)}, u32[]{:S(2)}, u32[]{:S(2)}) async-start(bf16[32,128,128]{2,1,0:T(8,128)(2,1)} %bitcast.117), calls=%async_computation.3 | async-start | bytes 2097152 | tf_op jit(solution)/shard_map/all_to_all | solution.py:125
  435.3 3.0 copy-start.4
  438.3 2.2 copy-start.1
  438.3 2.5 copy-start.5
  603.8 7.0 copy-start.3
  603.8 7.6 copy-start.15
  632.4 7.3 copy-start.9
  632.4 154.6 %all-to-all-start.5 = ((bf16[32,36,4096]{2,1,0:T(8,128)(2,1)}), bf16[32,36,4096]{2,1,0:T(8,128)(2,1)}, u32[]{:S(2)}, u32[]{:S(2)}) async-start(bf16[32,36,4096]{2,1,0:T(8,128)(2,1)} %reshape.196), calls=%async_computation.5 | async-start | bytes 20971520 | tf_op jit(solution)/shard_map/all_to_all | solution.py:159
  811.3 10.9 %copy-start.2 = (f32[128,4096]{1,0:T(8,128)S(1)}, f32[128,4096]{1,0:T(8,128)}, u32[]{:S(2)}) copy-start(f32[128,4096]{1,0:T(8,128)} %copy.63) | copy-start | bytes 6291460
  811.3 10.9 %copy-start.6 = (bf16[128,4096]{1,0:T(8,128)(2,1)S(1)}, bf16[128,4096]{1,0:T(8,128)(2,1)}, u32[]{:S(2)}) copy-start(bf16[128,4096]{1,0:T(8,128)(2,1)} %param.20) | copy-start | bytes 3145732
  (68 other events, 39.2 us)
where the time goes:
time: 834 us; the launch traced here: 824 us
  matrix products  285 us (34%)
  waiting for transfers between devices  200 us (24%)
  blocking collectives  125 us (15%)
  local copies, waits for them, and re-layouts  116 us (14%)
  other arithmetic  48.4 us (6%)
  starting transfers between devices  33.3 us (4%)
  loops' own time  15.5 us (2%)
    dot_general x108, matrix products, block_scores(): lax.dot_general(q_block[:, first_col:first_col + map_width], k_block[:, f...  198 us
    all_to_all x1, waiting for transfers between devices, shards(): lax.all_to_all(parts_made, ('ctx', 'exp'), split_axis=0, concat_axis=0, t...  147 us
    all_to_all x1, blocking collectives, shards(): lax.all_to_all(outgoing, ('ctx', 'exp'), split_axis=0, concat_axis=0, til...  125 us
    dot_general x36, matrix products, accumulate(): jnp.dot(weights, v_block, preferred_element_type=jnp.float32)  72.7 us
    while x216, local copies, waits for them, and re-layouts  20.7 us
  transfers between devices with their start and end apart: 5, of which 5 were waited for; matrix products, arithmetic and copies ran while one was open for 1% of the time, Pallas kernels for 0%

commit v1 on v0

v1 whole, which is shorter than its diff:
```python
import functools
import math

import jax
import jax.numpy as jnp
from jax import lax
from jax.experimental import pallas as pl
from jax.experimental.pallas import tpu as pltpu
from jax.sharding import PartitionSpec as P

EPSILON = 1e-05
OUT_SCALE = 0.8
LOG2E = math.log2(math.e)
LOW = -1e30
LANES = 128
SLOTS = 40
MIB = 1024 * 1024
contract_last = (((1,), (1,)), ((), ()))
contract_first = (((0,), (0,)), ((), ()))


def attention_kernel(bq, bk, lam_ref, qkv_ref, o_ref, kk, vv, qq, acc, largest):
    sources, _, rows, width = qkv_ref.shape
    length = sources * rows
    half = width // 2
    step_index = pl.program_id(0)

    @pl.when(step_index == 0)
    def _():
        keys = qkv_ref[:, 1].reshape(length, width)
        kk[:, :width] = keys
        kk[:, width:] = keys
        vv[:, :width] = qkv_ref[:, 2].reshape(length, width)
        vv[:, width:] = jnp.ones((length, width), vv.dtype)

    per = bq // rows
    q = qkv_ref[pl.ds(step_index * per, per), 0].reshape(bq, width)
    q = q.astype(jnp.float32) * (LOG2E / math.sqrt(half))
    hi = q.astype(jnp.bfloat16)
    lo = (q - hi.astype(jnp.float32)).astype(jnp.bfloat16)
    first = lax.broadcasted_iota(jnp.int32, (bq, width), 1) < half
    zero = jnp.zeros((bq, width), jnp.bfloat16)
    qq[:bq, :width] = jnp.where(first, hi, zero)
    qq[:bq, width:] = jnp.where(first, lo, zero)
    qq[bq:, :width] = jnp.where(first, zero, hi)
    qq[bq:, width:] = jnp.where(first, zero, lo)
    acc[...] = jnp.zeros_like(acc)
    largest[...] = jnp.full_like(largest, LOW)

    def chunk(j, masked):
        s = lax.dot_general(
            qq[...], kk[pl.ds(j * bk, bk), :], contract_last, preferred_element_type=jnp.float32
        )
        if masked:
            row = step_index * bq + lax.broadcasted_iota(jnp.int32, (bq, bk), 0)
            col = j * bk + lax.broadcasted_iota(jnp.int32, (bq, bk), 1)
            allowed = col <= row
            s = jnp.where(jnp.concatenate([allowed, allowed], axis=0), s, LOW)
        old = largest[...]
        new = jnp.maximum(old, jnp.max(s, axis=1, keepdims=True))
        largest[...] = new
        shrink = jnp.exp2(old - new)
        raised = jnp.exp2(s - new[:, :1]).astype(jnp.bfloat16)
        part = jnp.dot(raised, vv[pl.ds(j * bk, bk), :], preferred_element_type=jnp.float32)
        acc[:, :width] = acc[:, :width] * shrink + part[:, :width]
        acc[:, width:] = acc[:, width:] * shrink + part[:, width:]

    full = (step_index * bq) // bk

    def body(j, carried):
        chunk(j, False)
        return carried

    lax.fori_loop(0, full, body, 0)
    chunk(full, True)
    one = acc[:bq, :width] / acc[:bq, width:]
    two = acc[bq:, :width] / acc[bq:, width:]
    mixed = one - lam_ref[0] * two
    mean = jnp.mean(mixed * mixed, axis=1, keepdims=True)
    out = (OUT_SCALE * mixed * lax.rsqrt(mean + EPSILON)).astype(o_ref.dtype)
    o_ref[...] = out.reshape(o_ref.shape)


def attention(qkv, lam, bq=512, bk=1024):
    sources, _, rows, width = qkv.shape
    length = sources * rows
    per = bq // rows
    return pl.pallas_call(
        functools.partial(attention_kernel, bq, bk),
        grid=(length // bq,),
        out_shape=jax.ShapeDtypeStruct((sources, rows, width), jnp.bfloat16),
        in_specs=[
            pl.BlockSpec(memory_space=pltpu.SMEM),
            pl.BlockSpec(memory_space=pltpu.VMEM),
        ],
        out_specs=pl.BlockSpec((per, rows, width), lambda i: (i, 0, 0)),
        scratch_shapes=[
            pltpu.VMEM((length, 2 * width), jnp.bfloat16),
            pltpu.VMEM((length, 2 * width), jnp.bfloat16),
            pltpu.VMEM((2 * bq, 2 * width), jnp.bfloat16),
            pltpu.VMEM((2 * bq, 2 * width), jnp.float32),
            pltpu.VMEM((2 * bq, width), jnp.float32),
        ],
        compiler_params=pltpu.CompilerParams(vmem_limit_bytes=48 * MIB),
        cost_estimate=pl.CostEstimate(
            flops=6 * length * length * width, bytes_accessed=4 * MIB, transcendentals=length * length
        ),
        name="attention",
    )(lam, qkv)


def attend_columns(res_ref, heads_ref, h):
    columns = slice(h * LANES, (h + 1) * LANES)
    return res_ref[:, columns].astype(jnp.float32) + heads_ref[h].astype(jnp.float32)


def route_kernel(res_ref, heads_ref, router_ref, routes_ref, cap_ref, buf_ref, gate_ref, normed):
    heads, tokens, width = heads_ref.shape
    experts = router_ref.shape[0]
    square = jnp.zeros((tokens, width), jnp.float32)
    for h in range(heads):
        block = attend_columns(res_ref, heads_ref, h)
        square = square + block * block
    mean = jnp.sum(square, axis=1, keepdims=True) / (heads * width)
    factor = lax.rsqrt(mean + EPSILON)
    for h in range(heads):
        block = attend_columns(res_ref, heads_ref, h)
        normed[:, h * width : (h + 1) * width] = (block * factor).astype(jnp.bfloat16)
    logits = lax.dot_general(
        router_ref[...], normed[...], contract_last, preferred_element_type=jnp.float32
    )
    sig = 1.0 / (1.0 + jnp.exp(-logits))
    expert = lax.broadcasted_iota(jnp.int32, (experts, tokens), 0)
    named = (routes_ref[0:1, :] == expert) | (routes_ref[1:2, :] == expert)
    picked = jnp.where(named, sig, 0.0)
    gates = picked / jnp.sum(picked, axis=0, keepdims=True)
    before = lax.broadcasted_iota(jnp.int32, (tokens, tokens), 0) < lax.broadcasted_iota(
        jnp.int32, (tokens, tokens), 1
    )
    position = jnp.dot(
        named.astype(jnp.bfloat16), before.astype(jnp.bfloat16), preferred_element_type=jnp.float32
    )
    kept = named & (position < cap_ref[...].astype(jnp.float32))
    position = jnp.where(kept, position, -1.0).astype(jnp.int32)
    slot = lax.broadcasted_iota(jnp.int32, (SLOTS, tokens), 0)
    chosen = [slot == position[e : e + 1, :] for e in range(experts)]
    one_hot = jnp.concatenate([jnp.where(c, 1.0, 0.0) for c in chosen], axis=0)
    gate_ref[...] = jnp.concatenate(
        [jnp.where(chosen[e], gates[e : e + 1, :], 0.0) for e in range(experts)], axis=0
    )
    one_hot = one_hot.astype(jnp.bfloat16)
    for h in range(0, heads * width, 512):
        buf_ref[:, h : h + 512] = jnp.dot(
            one_hot, normed[:, h : h + 512], preferred_element_type=jnp.float32
        ).astype(jnp.bfloat16)


def route(residual, heads, router, routes, capacity):
    tokens, width = residual.shape
    experts = router.shape[0]
    slots = experts * SLOTS
    return pl.pallas_call(
        route_kernel,
        out_shape=(
            jax.ShapeDtypeStruct((slots, width), jnp.bfloat16),
            jax.ShapeDtypeStruct((slots, tokens), jnp.float32),
        ),
        scratch_shapes=[pltpu.VMEM((tokens, width), jnp.bfloat16)],
        compiler_params=pltpu.CompilerParams(vmem_limit_bytes=48 * MIB),
        name="route",
    )(residual, heads, router, routes, capacity)


def expert_kernel(x_ref, gate_ref, up_ref, down_ref, o_ref, acc):
    group = pl.program_id(0)
    x = x_ref[...]
    gate_out = jnp.dot(x, gate_ref[...], preferred_element_type=jnp.float32)
    up_out = jnp.dot(x, up_ref[...], preferred_element_type=jnp.float32)
    hidden = (gate_out / (1.0 + jnp.exp(-gate_out)) * up_out).astype(jnp.bfloat16)
    width = x_ref.shape[1]
    for c in range(0, width, 512):
        part = lax.dot_general(
            hidden, down_ref[c : c + 512, :], contract_last, preferred_element_type=jnp.float32
        ).astype(jnp.bfloat16).astype(jnp.float32)

        @pl.when(group == 0)
        def _():
            acc[:, c : c + 512] = part

        @pl.when(group > 0)
        def _():
            acc[:, c : c + 512] += part

    @pl.when(group == pl.num_programs(0) - 1)
    def _():
        o_ref[...] = acc[...].astype(o_ref.dtype)


def expert(x, gate_w, up_w, down_w):
    rows, width = x.shape
    groups, _, hidden = gate_w.shape
    weight = pl.BlockSpec((None, width, hidden), lambda g: (g, 0, 0))
    return pl.pallas_call(
        expert_kernel,
        grid=(groups,),
        out_shape=jax.ShapeDtypeStruct((rows, width), jnp.bfloat16),
        in_specs=[pl.BlockSpec((rows, width), lambda g: (0, 0)), weight, weight, weight],
        out_specs=pl.BlockSpec((rows, width), lambda g: (0, 0)),
        scratch_shapes=[pltpu.VMEM((rows, width), jnp.float32)],
        compiler_params=pltpu.CompilerParams(vmem_limit_bytes=56 * MIB),
        cost_estimate=pl.CostEstimate(
            flops=6 * rows * width * hidden * groups, bytes_accessed=30 * MIB, transcendentals=rows * hidden * groups
        ),
        name="experts",
    )(x, gate_w, up_w, down_w)


def combine_kernel(res_ref, heads_ref, back_ref, gate_ref, o_ref):
    heads = heads_ref.shape[0]
    gates = gate_ref[...]
    hi = gates.astype(jnp.bfloat16)
    lo = (gates - hi.astype(jnp.float32)).astype(jnp.bfloat16)
    for h in range(heads):
        columns = slice(h * LANES, (h + 1) * LANES)
        back = back_ref[:, columns]
        total = lax.dot_general(hi, back, contract_first, preferred_element_type=jnp.float32)
        total += lax.dot_general(lo, back, contract_first, preferred_element_type=jnp.float32)
        o_ref[:, columns] = (attend_columns(res_ref, heads_ref, h) + total).astype(o_ref.dtype)


def combine(residual, heads, back, gates):
    return pl.pallas_call(
        combine_kernel,
        out_shape=jax.ShapeDtypeStruct(residual.shape, jnp.bfloat16),
        compiler_params=pltpu.CompilerParams(vmem_limit_bytes=48 * MIB),
        name="combine",
    )(residual, heads, back, gates)


def shards(
    queries, key_rows, value_rows, residual, lambdas, router, gate_proj, up_proj, down_proj, routes, capacity
):
    tokens, width = queries.shape
    experts = router.shape[1]
    gate_all = lax.all_gather(gate_proj[0], "exp")
    up_all = lax.all_gather(up_proj[0], "exp")
    down_all = lax.all_gather(down_proj[0], "exp")

    heads = lambdas.shape[0]
    qkv = jnp.stack([queries, key_rows, value_rows]).reshape(3, tokens, heads, LANES)
    qkv = lax.all_to_all(
        qkv.transpose(2, 0, 1, 3), ("ctx", "exp"), split_axis=0, concat_axis=0, tiled=True
    )
    lam = lax.dynamic_slice_in_dim(lambdas, lax.axis_index(("ctx", "exp")), 1)
    mixed = attention(qkv, lam)
    mixed = lax.all_to_all(mixed, ("ctx", "exp"), split_axis=0, concat_axis=0, tiled=True)

    buffer, gates = route(residual, mixed, router.T, routes.T, capacity.T)
    buffer = lax.all_to_all(
        buffer.reshape(experts, SLOTS, width), "ctx", split_axis=0, concat_axis=0, tiled=True
    )
    results = expert(buffer.reshape(experts * SLOTS, width), gate_all, up_all, down_all)
    back = lax.all_to_all(
        results.reshape(experts, SLOTS, width), "ctx", split_axis=0, concat_axis=0, tiled=True
    )
    return combine(residual, mixed, back.reshape(experts * SLOTS, width), gates)


def solution(mesh):
    rows = P(("dp", "ctx", "exp"), None)
    weights = P("ctx", None, "exp")
    placed = (rows, rows, rows, rows, P(), P(), weights, weights, weights, rows, rows)
    return jax.shard_map(shards, mesh=mesh, in_specs=placed, out_specs=rows, check_vma=False)
```

time: 834 us -> 391 us (0.47)
  matrix products: 285 us -> 0 us
  local copies, waits for them, and re-layouts: 116 us -> 7.31 us
  Pallas kernels: 0 us -> 104 us
  blocking collectives: 125 us -> 75.5 us
  other arithmetic: 48.4 us -> 3.29 us
  waiting for transfers between devices: 200 us -> 169 us
  starting transfers between devices: 33.3 us -> 15.7 us
  loops' own time: 15.5 us -> 0 us
  between operations: 0.52 us -> 13.2 us
    dot_general x148 -> x0, matrix products: 285 us -> none  [the longest x108 198 us: block_scores(): lax.dot_general(q_block[:, first_col:first_col + map_width], k_block[:, f...]
    all_to_all x5 -> x2, waiting for transfers between devices: 200 us -> 58.2 us  [the longest x1 42.8 us: shards(): lax.all_to_all(qkv.transpose(2, 0, 1, 3), ('ctx', 'exp'), split_axis=0, c...]
    all_gather x0 -> x3, waiting for transfers between devices: none -> 108 us  [the longest x1 88.5 us: shards(): down_all = lax.all_gather(down_proj[0], 'exp')]
    pallas_call x0 -> x4, Pallas kernels: none -> 104 us  [the longest x1 76.4 us: attention(): pl.pallas_call(functools.partial(attention_kernel, bq, bk), grid=(length...]
    all_to_all x1 -> x2, blocking collectives: 125 us -> 75.5 us  [the longest x1 38 us: shards(): lax.all_to_all(buffer.reshape(experts, SLOTS, width), 'ctx', split_axis=0...]
    reduce_sum x85 -> x0, other arithmetic: 36.8 us -> none  [the longest x72 14.2 us: gather_stats(): jnp.sum(jnp.exp(both_maps[map_index] - new_largest[:, None]), axis=1)]
    reshape x4 -> x0, local copies, waits for them, and re-layouts: 34.6 us -> none  [the longest x1 13.3 us: shards(): parts_made = expert_part(arrived.reshape(-1, width), gate_w, up_w, down_w)]
    while x216 -> x0, local copies, waits for them, and re-layouts: 20.7 us -> none
  transfers between devices with their start and end apart: 5 -> 5, of which waited for: 5 -> 4; matrix products, arithmetic and copies ran while one was open for 1% -> 3% of each run, Pallas kernels for 0% -> 20%
where the time goes in v1:
time: 391 us; the launch traced here: 387 us
  waiting for transfers between devices  169 us (43%)
  Pallas kernels  104 us (27%)
  blocking collectives  75.5 us (19%)
  starting transfers between devices  15.7 us (4%)
  between operations  13.2 us (3%)
  local copies, waits for them, and re-layouts  7.31 us (2%)
    all_gather x1, waiting for transfers between devices, shards(): down_all = lax.all_gather(down_proj[0], 'exp')  88.5 us
    pallas_call x1, Pallas kernels, attention(): pl.pallas_call(functools.partial(attention_kernel, bq, bk), grid=(length...  76.4 us
    all_to_all x1, waiting for transfers between devices, shards(): lax.all_to_all(qkv.transpose(2, 0, 1, 3), ('ctx', 'exp'), split_axis=0, c...  42.8 us
    all_to_all x1, blocking collectives, shards(): lax.all_to_all(buffer.reshape(experts, SLOTS, width), 'ctx', split_axis=0...  38 us
    all_to_all x1, blocking collectives, shards(): lax.all_to_all(results.reshape(experts, SLOTS, width), 'ctx', split_axis=...  37.5 us
    pallas_call x1, Pallas kernels, expert(): pl.pallas_call(expert_kernel, grid=(groups,), out_shape=jax.ShapeDtypeStr...  22.9 us
    all_gather x1, waiting for transfers between devices, shards(): up_all = lax.all_gather(up_proj[0], 'exp')  19.9 us
    all_to_all x1, waiting for transfers between devices, shards(): lax.all_to_all(mixed, ('ctx', 'exp'), split_axis=0, concat_axis=0, tiled=...  15.3 us
  transfers between devices with their start and end apart: 5, of which 4 were waited for; matrix products, arithmetic and copies ran while one was open for 3% of the time, Pallas kernels for 20%

profile of v1, /device:TPU:120, one launch (start us, length us, event | category | flops | bytes accessed | tf_op | source)
XLA Modules:
  0.0 387.3 jit_solution(10042025759302946263)
XLA Ops:
  6.5 0.7 all-gather.4.cloned.1.call-update
  7.3 0.7 all-gather.6.cloned.1.call-update
  8.1 0.7 all-gather.8.cloned.1.call-update
  8.8 0.7 copy.20
  9.4 0.7 copy.23
  10.1 1.6 copy.21
  11.7 0.7 copy.24
  12.4 1.6 copy.22
  14.0 1.3 copy.25
  15.3 3.3 maximum_bitcast_fusion
  18.6 7.5 %all-to-all-start = ((bf16[32,3,128,128]{3,2,1,0:T(8,128)(2,1)}), bf16[32,3,128,128]{3,2,1,0:T(8,128)(2,1)}, u32[]{:S(2)}, u32[]{:S(2)}) async-start(bf16[32,3,128,128]{3,2,1,0:T(8,128)(2,1)} %maximum_bitcast_fusion), calls=%async_computation | async-start | bytes 6291456 | tf_op jit(solution)/shard_map/all_to_all | solution.py:251
  26.1 0.7 dynamic_slice.3.lam_ref
  26.8 42.8 %all-to-all-done.qkv_ref = bf16[32,3,128,128]{3,2,1,0:T(8,128)(2,1)} async-done(((bf16[32,3,128,128]{3,2,1,0:T(8,128)(2,1)}), bf16[32,3,128,128]{3,2,1,0:T(8,128)(2,1)}, u32[]{:S(2)}, u32[]{:S(2)}) %all-to-all-start) | async-done | bytes 3145760 | tf_op jit(solution)/shard_map/all_to_all | solution.py:251
  69.7 76.4 %attention.1 = bf16[32,128,128]{2,1,0:T(8,128)(2,1)} custom-call(f32[1]{0:T(128)} %dynamic_slice.3.lam_ref, bf16[32,3,128,128]{3,2,1,0:T(8,128)(2,1)} %all-to-all-done.qkv_ref), custom_call_target="tpu_custom_call" | custom-call | flops 12884901888 | bytes 4194304 | tf_op jit(solution)/shard_map/attention/pallas_call | solution.py:88
  146.0 8.2 %all-to-all-start.1 = ((bf16[32,128,128]{2,1,0:T(8,128)(2,1)}), bf16[32,128,128]{2,1,0:T(8,128)(2,1)S(1)}, u32[]{:S(2)}, u32[]{:S(2)}) async-start(bf16[32,128,128]{2,1,0:T(8,128)(2,1)} %attention.1), calls=%async_computation.1 | async-start | bytes 2097152 | tf_op jit(solution)/shard_map/all_to_all | solution.py:256
  154.2 0.1 copy.26.cap_ref
  154.3 15.3 %all-to-all-done.1.heads_ref = bf16[32,128,128]{2,1,0:T(8,128)(2,1)S(1)} async-done(((bf16[32,128,128]{2,1,0:T(8,128)(2,1)}), bf16[32,128,128]{2,1,0:T(8,128)(2,1)S(1)}, u32[]{:S(2)}, u32[]{:S(2)}) %all-to-all-start.1) | async-done | bytes 1048608 | tf_op jit(solution)/shard_map/all_to_all | solution.py:256
  169.6 1.5 route.1
  171.2 38.0 %all_to_all.20 = bf16[8,40,4096]{2,1,0:T(8,128)(2,1)} all-to-all(bf16[8,40,4096]{2,1,0:T(8,128)(2,1)S(1)} %bitcast.13), channel_id=1, replica_groups=mesh['dp'=8,'ctx'=8,'exp'=4] {'ctx'}, dimensions={0} | all-to-all | bytes 5242880 | tf_op jit(solution)/shard_map/all_to_all | solution.py:259
  209.2 19.9 %all-gather.6.cloned.1.call-done.up_ref = bf16[4,4096,256]{2,1,0:T(8,128)(2,1)} async-done(((bf16[1,4096,256]{2,1,0:T(8,128)(2,1)}), bf16[4,4096,256]{2,1,0:T(8,128)(2,1)}) %all-gather.6.cloned.1.call-update) | async-done | bytes 8388624 | tf_op jit(solution)/shard_map/all_gather | solution.py:246
  229.1 88.5 %all-gather.8.cloned.1.call-done.down_ref = bf16[4,4096,256]{2,1,0:T(8,128)(2,1)} async-done(((bf16[1,4096,256]{2,1,0:T(8,128)(2,1)}), bf16[4,4096,256]{2,1,0:T(8,128)(2,1)}) %all-gather.8.cloned.1.call-update) | async-done | bytes 8388624 | tf_op jit(solution)/shard_map/all_gather | solution.py:247
  317.6 22.9 %experts.1 = bf16[320,4096]{1,0:T(8,128)(2,1)} custom-call(bf16[320,4096]{1,0:T(8,128)(2,1)} %bitcast.16, bf16[4,4096,256]{2,1,0:T(8,128)(2,1)} %all-gather.4.cloned.1.call-done.gate_ref, bf16[4,4096,256]{2,1,0:T(8,128)(2,1)} %all-gather.6.cloned.1.call-done.up_ref, bf16[4,4096,256]{2,1,0:T(8,128)(2,1)} %all-gather.8.cloned.1.call-done.down_ref), custom_call_target="tpu_custom_call" | custom-call | flops 8053063680 | bytes 31457280 | tf_op jit(solution)/shard_map/experts/pallas_call | solution.py:203
  340.5 37.5 %all_to_all.21 = bf16[8,40,4096]{2,1,0:T(8,128)(2,1)S(1)} all-to-all(bf16[8,40,4096]{2,1,0:T(8,128)(2,1)} %bitcast.17), channel_id=1, replica_groups=mesh['dp'=8,'ctx'=8,'exp'=4] {'ctx'}, dimensions={0} | all-to-all | bytes 5242880 | tf_op jit(solution)/shard_map/all_to_all | solution.py:263
  378.0 2.8 combine.1
  (16 shorter events, 0.1 us)
Async XLA Ops:
  6.5 2.2 copy-start.3
  6.5 202.7 %all-gather.4.cloned.1.call-start = ((), (), s32[]{:S(2)}) async-start(), calls=%async_computation.4 | async-start | bytes 10485760 | tf_op jit(solution)/shard_map/all_gather | solution.py:245
  7.3 221.8 %all-gather.6.cloned.1.call-start = ((), (), s32[]{:S(2)}) async-start(), calls=%async_computation.5 | async-start | bytes 10485760 | tf_op jit(solution)/shard_map/all_gather | solution.py:246
  8.0 309.6 %all-gather.8.cloned.1.call-start = ((), (), s32[]{:S(2)}) async-start(), calls=%async_computation.6 | async-start | bytes 10485760 | tf_op jit(solution)/shard_map/all_gather | solution.py:247
  18.6 7.5 %copy-start.5 = (f32[32]{0:T(128)S(1)}, f32[32]{0:T(128)}, u32[]{:S(2)}) copy-start(f32[32]{0:T(128)} %param.15) | copy-start | bytes 388
  18.6 51.0 %all-to-all-start = ((bf16[32,3,128,128]{3,2,1,0:T(8,128)(2,1)}), bf16[32,3,128,128]{3,2,1,0:T(8,128)(2,1)}, u32[]{:S(2)}, u32[]{:S(2)}) async-start(bf16[32,3,128,128]{3,2,1,0:T(8,128)(2,1)} %maximum_bitcast_fusion), calls=%async_computation | async-start | bytes 6291456 | tf_op jit(solution)/shard_map/all_to_all | solution.py:251
  26.8 127.4 %copy-start.4 = (s32[1,8]{1,0:T(1,128)S(1)}, s32[1,8]{1,0:T(1,128)}, u32[]{:S(2)}) copy-start(s32[1,8]{1,0:T(1,128)} %param.21) | copy-start | bytes 100
  26.8 142.8 %copy-start = (bf16[128,4096]{1,0:T(8,128)(2,1)S(1)}, bf16[128,4096]{1,0:T(8,128)(2,1)}, u32[]{:S(2)}) copy-start(bf16[128,4096]{1,0:T(8,128)(2,1)} %res_ref.3) | copy-start | bytes 3145732
  26.8 142.8 %copy-start.1 = (bf16[4096,8]{0,1:T(8,128)(2,1)S(1)}, bf16[4096,8]{0,1:T(8,128)(2,1)}, u32[]{:S(2)}) copy-start(bf16[4096,8]{0,1:T(8,128)(2,1)} %param.16) | copy-start | bytes 196612
  26.8 142.8 %copy-start.2 = (s32[128,2]{0,1:T(2,128)S(1)}, s32[128,2]{0,1:T(2,128)}, u32[]{:S(2)}) copy-start(s32[128,2]{0,1:T(2,128)} %param.20) | copy-start | bytes 3076
  146.0 23.6 %all-to-all-start.1 = ((bf16[32,128,128]{2,1,0:T(8,128)(2,1)}), bf16[32,128,128]{2,1,0:T(8,128)(2,1)S(1)}, u32[]{:S(2)}, u32[]{:S(2)}) async-start(bf16[32,128,128]{2,1,0:T(8,128)(2,1)} %attention.1), calls=%async_computation.1 | async-start | bytes 2097152 | tf_op jit(solution)/shard_map/all_to_all | solution.py:256
Sparse Core Ops, SparseCore 0:
  9.2 119.8 all-gather.3
  130.9 98.1 all-gather.5
  230.9 86.6 all-gather.7

commit v2 on v1

v2 whole, which is shorter than its diff:
```python
import functools
import math

import jax
import jax.numpy as jnp
from jax import lax
from jax.experimental import pallas as pl
from jax.experimental.pallas import tpu as pltpu
from jax.sharding import PartitionSpec as P

EPSILON = 1e-05
OUT_SCALE = 0.8
LOG2E = math.log2(math.e)
LOW = -1e30
LANES = 128
SLOTS = 40
MIB = 1024 * 1024
MESH = pl.DeviceIdType.MESH
contract_last = (((1,), (1,)), ((), ()))
contract_first = (((0,), (0,)), ((), ()))


def relative(ctx=0, exp=0, dp=0):
    def place(axis, step):
        size = lax.axis_size(axis)
        return lax.rem(lax.axis_index(axis) + step + size, size)

    return {"dp": place("dp", dp), "ctx": place("ctx", ctx), "exp": place("exp", exp)}


def front_kernel(
    bq, bk, lam_ref, q_ref, k_ref, v_ref, gate_ref, up_ref, down_ref, heads_ref, gate_all, up_all, down_all,
    qkv, mixed, kk, vv, qq, acc, largest, qkv_send, qkv_recv, out_send, out_recv, w_send, w_recv,
):
    _, sources, rows, width = qkv.shape
    length = sources * rows
    half = width // 2
    fan = lax.axis_size("exp")
    me = lax.axis_index("ctx") * fan + lax.axis_index("exp")
    parity = lax.rem(lax.axis_index("dp"), 2)

    def member(index):
        return {"dp": lax.axis_index("dp"), "ctx": lax.div(index, fan), "exp": lax.rem(index, fan)}

    barrier = pltpu.get_barrier_semaphore()

    def greet(step, carried):
        pl.semaphore_signal(
            barrier, inc=1, device_id=member(lax.rem(me + step, sources)), device_id_type=MESH
        )
        return carried

    lax.fori_loop(1, sources, greet, 0)
    pl.semaphore_signal(barrier, inc=1, device_id=relative(dp=1), device_id_type=MESH)
    pl.semaphore_signal(barrier, inc=1, device_id=relative(dp=-1), device_id_type=MESH)
    pl.semaphore_wait(barrier, sources + 1)

    inputs = (q_ref, k_ref, v_ref)

    def send_heads(step, carried):
        target = lax.rem(me + step, sources)
        columns = pl.ds(pl.multiple_of(target * width, width), width)
        for which in range(3):
            pltpu.make_async_remote_copy(
                src_ref=inputs[which].at[:, columns],
                dst_ref=qkv.at[which, me],
                send_sem=qkv_send,
                recv_sem=qkv_recv,
                device_id=member(target),
                device_id_type=MESH,
            ).start()
        return carried

    lax.fori_loop(1, sources, send_heads, 0)
    own = pl.ds(pl.multiple_of(me * width, width), width)
    for which in range(3):
        pltpu.make_async_copy(inputs[which].at[:, own], qkv.at[which, me], qkv_recv).start()

    weights = (gate_ref, up_ref, down_ref)
    gathered = (gate_all, up_all, down_all)
    quarter = gate_ref.shape[0] // 4

    def chunk_rows(which_half, part):
        return pl.ds(pl.multiple_of((which_half * 2 + part) * quarter, quarter), quarter)

    def transfer(array, slot, part, along_dp, src, forward):
        ways = relative(dp=1 if part == 0 else -1) if along_dp else relative(exp=1 if forward else -1)
        number = ((array * 3 + slot) * 2 + part) * 2 + (1 if along_dp else 0)
        return pltpu.make_async_remote_copy(
            src_ref=src,
            dst_ref=gathered[array].at[slot, chunk_rows(parity, part)],
            send_sem=w_send.at[number],
            recv_sem=w_recv.at[number],
            device_id=ways,
            device_id_type=MESH,
        )

    def arrived(array, slot, part, along_dp):
        number = ((array * 3 + slot) * 2 + part) * 2 + (1 if along_dp else 0)
        rows_here = chunk_rows(1 - parity if along_dp else parity, part)
        block = gathered[array].at[slot, rows_here]
        pltpu.make_async_copy(block, block, w_recv.at[number]).wait()

    def own_copy(array, slot, part):
        return transfer(
            array, slot, part, False, weights[array].at[chunk_rows(parity, part)], slot == 1
        )

    def across(array, part):
        slot = 1 if part == 0 else 0
        return transfer(
            array, 2, part, False, gathered[array].at[slot, chunk_rows(parity, part)], part == 0
        )

    def along(array, slot, part):
        return transfer(
            array, slot, part, True, gathered[array].at[slot, chunk_rows(parity, part)], None
        )

    def first(array):
        for part in range(2):
            own_copy(array, 1, part).start()
            own_copy(array, 0, 1 - part).start()

    def second(array):
        arrived(array, 1, 0, False)
        across(array, 0).start()
        along(array, 1, 0).start()
        arrived(array, 0, 1, False)
        across(array, 1).start()
        along(array, 0, 1).start()
        arrived(array, 1, 1, False)
        along(array, 1, 1).start()
        arrived(array, 0, 0, False)
        along(array, 0, 0).start()

    def third(array):
        arrived(array, 2, 0, False)
        along(array, 2, 0).start()
        arrived(array, 2, 1, False)
        along(array, 2, 1).start()

    def last(array):
        for slot in range(3):
            for part in range(2):
                arrived(array, slot, part, True)
                along(array, slot, part).wait_send()
        for part in range(2):
            own_copy(array, 0, part).wait_send()
            own_copy(array, 1, part).wait_send()
            across(array, part).wait_send()

    first(0)
    first(1)

    pltpu.make_async_copy(qkv, qkv, qkv_recv).wait()
    keys = qkv[1].reshape(length, width)
    kk[:, :width] = keys
    kk[:, width:] = keys
    vv[:, :width] = qkv[2].reshape(length, width)
    vv[:, width:] = jnp.ones((length, width), vv.dtype)

    per = bq // rows
    lam = lam_ref[me]

    def query_block(i, carried):
        @pl.when(i == 2)
        def _():
            second(0)
            first(2)

        @pl.when(i == 4)
        def _():
            third(0)

        @pl.when(i == 5)
        def _():
            second(1)

        @pl.when(i == 6)
        def _():
            third(1)

        q = qkv[0, pl.ds(i * per, per)].reshape(bq, width)
        q = q.astype(jnp.float32) * (LOG2E / math.sqrt(half))
        hi = q.astype(jnp.bfloat16)
        lo = (q - hi.astype(jnp.float32)).astype(jnp.bfloat16)
        lower = lax.broadcasted_iota(jnp.int32, (bq, width), 1) < half
        zero = jnp.zeros((bq, width), jnp.bfloat16)
        qq[:bq, :width] = jnp.where(lower, hi, zero)
        qq[:bq, width:] = jnp.where(lower, lo, zero)
        qq[bq:, :width] = jnp.where(lower, zero, hi)
        qq[bq:, width:] = jnp.where(lower, zero, lo)
        acc[...] = jnp.zeros_like(acc)
        largest[...] = jnp.full_like(largest, LOW)

        def chunk(j, masked):
            keys_here = pl.ds(pl.multiple_of(j * bk, bk), bk)
            s = lax.dot_general(
                qq[...], kk[keys_here, :], contract_last, preferred_element_type=jnp.float32
            )
            if masked:
                row = i * bq + lax.broadcasted_iota(jnp.int32, (bq, bk), 0)
                col = j * bk + lax.broadcasted_iota(jnp.int32, (bq, bk), 1)
                allowed = col <= row
                s = jnp.where(jnp.concatenate([allowed, allowed], axis=0), s, LOW)
            old = largest[...]
            new = jnp.maximum(old, jnp.max(s, axis=1, keepdims=True))
            largest[...] = new
            shrink = jnp.exp2(old - new)
            raised = jnp.exp2(s - new[:, :1]).astype(jnp.bfloat16)
            part = jnp.dot(raised, vv[keys_here, :], preferred_element_type=jnp.float32)
            acc[:, :width] = acc[:, :width] * shrink + part[:, :width]
            acc[:, width:] = acc[:, width:] * shrink + part[:, width:]

        full = lax.div(i * bq, bk)

        def body(j, inner):
            chunk(j, False)
            return inner

        lax.fori_loop(0, full, body, 0)
        chunk(full, True)
        one = acc[:bq, :width] / acc[:bq, width:]
        two = acc[bq:, :width] / acc[bq:, width:]
        blend = one - lam * two
        mean = jnp.mean(blend * blend, axis=1, keepdims=True)
        out = (OUT_SCALE * blend * lax.rsqrt(mean + EPSILON)).astype(mixed.dtype)
        mixed[pl.ds(i * per, per)] = out.reshape(per, rows, width)

        def send_rows(r, inner):
            target = i * per + r

            @pl.when(target != me)
            def _():
                pltpu.make_async_remote_copy(
                    src_ref=mixed.at[target],
                    dst_ref=heads_ref.at[me],
                    send_sem=out_send,
                    recv_sem=out_recv,
                    device_id=member(target),
                    device_id_type=MESH,
                ).start()

            @pl.when(target == me)
            def _():
                pltpu.make_async_copy(mixed.at[target], heads_ref.at[me], out_recv).start()

            return inner

        lax.fori_loop(0, per, send_rows, 0)
        return carried

    lax.fori_loop(0, length // bq, query_block, 0)
    second(2)
    third(2)
    others = pl.ds(0, sources - 1)
    for which in range(3):
        pltpu.make_async_copy(qkv.at[which, others], qkv.at[which, others], qkv_send).wait()
    pltpu.make_async_copy(mixed.at[others], mixed.at[others], out_send).wait()
    pltpu.make_async_copy(heads_ref, heads_ref, out_recv).wait()
    for array in range(3):
        last(array)


def front(lambdas, queries, key_rows, value_rows, gate_w, up_w, down_w, bq=512, bk=1024):
    rows, total = queries.shape
    width = LANES
    heads = total // width
    length = heads * rows
    anywhere = pl.BlockSpec(memory_space=pl.ANY)
    others = jax.ShapeDtypeStruct((lax.axis_size("exp") - 1, *gate_w.shape), gate_w.dtype)
    copies = 3 * 3 * 2 * 2
    return pl.pallas_call(
        functools.partial(front_kernel, bq, bk),
        out_shape=(jax.ShapeDtypeStruct((heads, rows, width), jnp.bfloat16), others, others, others),
        in_specs=[pl.BlockSpec(memory_space=pltpu.SMEM)] + [anywhere] * 6,
        out_specs=(anywhere,) * 4,
        scratch_shapes=[
            pltpu.VMEM((3, heads, rows, width), jnp.bfloat16),
            pltpu.VMEM((heads, rows, width), jnp.bfloat16),
            pltpu.VMEM((length, 2 * width), jnp.bfloat16),
            pltpu.VMEM((length, 2 * width), jnp.bfloat16),
            pltpu.VMEM((2 * bq, 2 * width), jnp.bfloat16),
            pltpu.VMEM((2 * bq, 2 * width), jnp.float32),
            pltpu.VMEM((2 * bq, width), jnp.float32),
            pltpu.SemaphoreType.DMA,
            pltpu.SemaphoreType.DMA,
            pltpu.SemaphoreType.DMA,
            pltpu.SemaphoreType.DMA,
            pltpu.SemaphoreType.DMA((copies,)),
            pltpu.SemaphoreType.DMA((copies,)),
        ],
        compiler_params=pltpu.CompilerParams(
            vmem_limit_bytes=56 * MIB, collective_id=0, has_side_effects=True
        ),
        name="front",
    )(lambdas, queries, key_rows, value_rows, gate_w, up_w, down_w)


def attend_columns(res_ref, heads_ref, h):
    columns = slice(h * LANES, (h + 1) * LANES)
    return res_ref[:, columns].astype(jnp.float32) + heads_ref[h].astype(jnp.float32)


def route_kernel(res_ref, heads_ref, router_ref, routes_ref, cap_ref, buf_ref, gate_ref, normed):
    heads, tokens, width = heads_ref.shape
    experts = router_ref.shape[0]
    square = jnp.zeros((tokens, width), jnp.float32)
    for h in range(heads):
        block = attend_columns(res_ref, heads_ref, h)
        square = square + block * block
    mean = jnp.sum(square, axis=1, keepdims=True) / (heads * width)
    factor = lax.rsqrt(mean + EPSILON)
    for h in range(heads):
        block = attend_columns(res_ref, heads_ref, h)
        normed[:, h * width : (h + 1) * width] = (block * factor).astype(jnp.bfloat16)
    logits = lax.dot_general(
        router_ref[...], normed[...], contract_last, preferred_element_type=jnp.float32
    )
    sig = 1.0 / (1.0 + jnp.exp(-logits))
    expert = lax.broadcasted_iota(jnp.int32, (experts, tokens), 0)
    named = (routes_ref[0:1, :] == expert) | (routes_ref[1:2, :] == expert)
    picked = jnp.where(named, sig, 0.0)
    gates = picked / jnp.sum(picked, axis=0, keepdims=True)
    before = lax.broadcasted_iota(jnp.int32, (tokens, tokens), 0) < lax.broadcasted_iota(
        jnp.int32, (tokens, tokens), 1
    )
    position = jnp.dot(
        named.astype(jnp.bfloat16), before.astype(jnp.bfloat16), preferred_element_type=jnp.float32
    )
    kept = named & (position < cap_ref[...].astype(jnp.float32))
    position = jnp.where(kept, position, -1.0).astype(jnp.int32)
    slot = lax.broadcasted_iota(jnp.int32, (SLOTS, tokens), 0)
    chosen = [slot == position[e : e + 1, :] for e in range(experts)]
    one_hot = jnp.concatenate([jnp.where(c, 1.0, 0.0) for c in chosen], axis=0)
    gate_ref[...] = jnp.concatenate(
        [jnp.where(chosen[e], gates[e : e + 1, :], 0.0) for e in range(experts)], axis=0
    )
    one_hot = one_hot.astype(jnp.bfloat16)
    for h in range(0, heads * width, 512):
        buf_ref[:, h : h + 512] = jnp.dot(
            one_hot, normed[:, h : h + 512], preferred_element_type=jnp.float32
        ).astype(jnp.bfloat16)


def route(residual, heads, router, routes, capacity):
    tokens, width = residual.shape
    experts = router.shape[0]
    slots = experts * SLOTS
    return pl.pallas_call(
        route_kernel,
        out_shape=(
            jax.ShapeDtypeStruct((slots, width), jnp.bfloat16),
            jax.ShapeDtypeStruct((slots, tokens), jnp.float32),
        ),
        scratch_shapes=[pltpu.VMEM((tokens, width), jnp.bfloat16)],
        compiler_params=pltpu.CompilerParams(vmem_limit_bytes=48 * MIB),
        name="route",
    )(residual, heads, router, routes, capacity)


def expert_kernel(x_ref, gate_own, up_own, down_own, gate_ref, up_ref, down_ref, o_ref, acc):
    group = pl.program_id(0)
    width = x_ref.shape[1]

    def contribute(gate_w, up_w, down_w, begin):
        x = x_ref[...]
        gate_out = jnp.dot(x, gate_w[...], preferred_element_type=jnp.float32)
        up_out = jnp.dot(x, up_w[...], preferred_element_type=jnp.float32)
        hidden = (gate_out / (1.0 + jnp.exp(-gate_out)) * up_out).astype(jnp.bfloat16)
        for c in range(0, width, 512):
            part = lax.dot_general(
                hidden, down_w[c : c + 512, :], contract_last, preferred_element_type=jnp.float32
            ).astype(jnp.bfloat16).astype(jnp.float32)
            if begin:
                acc[:, c : c + 512] = part
            else:
                acc[:, c : c + 512] += part

    @pl.when(group == 0)
    def _():
        contribute(gate_own, up_own, down_own, True)

    @pl.when(group > 0)
    def _():
        contribute(gate_ref, up_ref, down_ref, False)

    @pl.when(group == pl.num_programs(0) - 1)
    def _():
        o_ref[...] = acc[...].astype(o_ref.dtype)


def expert(x, own, others):
    rows, width = x.shape
    groups, _, hidden = others[0].shape
    groups += 1
    whole = pl.BlockSpec((width, hidden), lambda g: (0, 0), pipeline_mode=pl.Buffered(1))
    weight = pl.BlockSpec((None, width, hidden), lambda g: (jnp.maximum(g - 1, 0), 0, 0))
    return pl.pallas_call(
        expert_kernel,
        grid=(groups,),
        out_shape=jax.ShapeDtypeStruct((rows, width), jnp.bfloat16),
        in_specs=[pl.BlockSpec((rows, width), lambda g: (0, 0))] + [whole] * 3 + [weight] * 3,
        out_specs=pl.BlockSpec((rows, width), lambda g: (0, 0)),
        scratch_shapes=[pltpu.VMEM((rows, width), jnp.float32)],
        compiler_params=pltpu.CompilerParams(vmem_limit_bytes=56 * MIB),
        name="experts",
    )(x, *own, *others)


def combine_kernel(res_ref, heads_ref, back_ref, gate_ref, o_ref):
    heads = heads_ref.shape[0]
    gates = gate_ref[...]
    hi = gates.astype(jnp.bfloat16)
    lo = (gates - hi.astype(jnp.float32)).astype(jnp.bfloat16)
    for h in range(heads):
        columns = slice(h * LANES, (h + 1) * LANES)
        back = back_ref[:, columns]
        total = lax.dot_general(hi, back, contract_first, preferred_element_type=jnp.float32)
        total += lax.dot_general(lo, back, contract_first, preferred_element_type=jnp.float32)
        o_ref[:, columns] = (attend_columns(res_ref, heads_ref, h) + total).astype(o_ref.dtype)


def combine(residual, heads, back, gates):
    return pl.pallas_call(
        combine_kernel,
        out_shape=jax.ShapeDtypeStruct(residual.shape, jnp.bfloat16),
        compiler_params=pltpu.CompilerParams(vmem_limit_bytes=48 * MIB),
        name="combine",
    )(residual, heads, back, gates)


def shards(
    queries, key_rows, value_rows, residual, lambdas, router, gate_proj, up_proj, down_proj, routes, capacity
):
    tokens, width = queries.shape
    experts = router.shape[1]
    own = (gate_proj[0], up_proj[0], down_proj[0])
    mixed, *others = front(lambdas, queries, key_rows, value_rows, *own)

    buffer, gates = route(residual, mixed, router.T, routes.T, capacity.T)
    buffer = lax.all_to_all(
        buffer.reshape(experts, SLOTS, width), "ctx", split_axis=0, concat_axis=0, tiled=True
    )
    results = expert(buffer.reshape(experts * SLOTS, width), own, others)
    back = lax.all_to_all(
        results.reshape(experts, SLOTS, width), "ctx", split_axis=0, concat_axis=0, tiled=True
    )
    return combine(residual, mixed, back.reshape(experts * SLOTS, width), gates)


def solution(mesh):
    rows = P(("dp", "ctx", "exp"), None)
    weights = P("ctx", None, "exp")
    placed = (rows, rows, rows, rows, P(), P(), weights, weights, weights, rows, rows)
    return jax.shard_map(shards, mesh=mesh, in_specs=placed, out_specs=rows, check_vma=False)
```

time: 391 us -> 314 us (0.80)
  waiting for transfers between devices: 169 us -> 0 us
  Pallas kernels: 104 us -> 232 us
  starting transfers between devices: 15.7 us -> 0 us
  between operations: 13.2 us -> 0.05 us
  local copies, waits for them, and re-layouts: 7.31 us -> 1.96 us
    pallas_call x1, Pallas kernels: 76.4 us -> 211 us  [front(): pl.pallas_call(functools.partial(front_kernel, bq, bk), out_shape=(jax.Sh...]
    all_gather x3 -> x0, waiting for transfers between devices: 108 us -> none  [the longest x1 88.5 us: shards(): down_all = lax.all_gather(down_proj[0], 'exp')]
    all_to_all x2 -> x0, waiting for transfers between devices: 58.2 us -> none  [the longest x1 42.8 us: shards(): lax.all_to_all(qkv.transpose(2, 0, 1, 3), ('ctx', 'exp'), split_axis=0, c...]
    all_to_all x2 -> x0, starting transfers between devices: 15.6 us -> none  [the longest x1 8.16 us: shards(): lax.all_to_all(mixed, ('ctx', 'exp'), split_axis=0, concat_axis=0, tiled=...]
    pallas_call x1, Pallas kernels: 22.9 us -> 17.1 us  [expert(): pl.pallas_call(expert_kernel, grid=(groups,), out_shape=jax.ShapeDtypeStr...]
  transfers between devices with their start and end apart: 5 -> 0, of which waited for: 4 -> 0; matrix products, arithmetic and copies ran while one was open for 3% -> 0% of each run, Pallas kernels for 20% -> 0%
where the time goes in v2:
time: 314 us; the launch traced here: 310 us
  Pallas kernels  232 us (74%)
  blocking collectives  76.2 us (24%)
    pallas_call x1, Pallas kernels, front(): pl.pallas_call(functools.partial(front_kernel, bq, bk), out_shape=(jax.Sh...  211 us
    all_to_all x1, blocking collectives, shards(): lax.all_to_all(buffer.reshape(experts, SLOTS, width), 'ctx', split_axis=0...  39.3 us
    all_to_all x1, blocking collectives, shards(): lax.all_to_all(results.reshape(experts, SLOTS, width), 'ctx', split_axis=...  36.9 us
    pallas_call x1, Pallas kernels, expert(): pl.pallas_call(expert_kernel, grid=(groups,), out_shape=jax.ShapeDtypeStr...  17.1 us

profile of v2, /device:TPU:120, one launch (start us, length us, event | category | flops | bytes accessed | tf_op | source)
XLA Modules:
  0.0 310.4 jit_solution(1393574354378991082)
XLA Ops:
  0.0 0.7 copy.12.cap_ref
  0.7 0.0 copy-start
  0.7 0.0 copy-start.3
  0.7 0.0 copy-start.4
  0.7 210.8 %front.1 = (bf16[32,128,128]{2,1,0:T(8,128)(2,1)}, bf16[3,4096,256]{2,1,0:T(8,128)(2,1)}, bf16[3,4096,256]{2,1,0:T(8,128)(2,1)}, bf16[3,4096,256]{2,1,0:T(8,128)(2,1)}) custom-call(f32[32]{0:T(128)} %lam_ref.1, bf16[128,4096]{1,0:T(8,128)(2,1)} %q_ref.1, bf16[128,4096]{1,0:T(8,128)(2,1)} %k_ref.1, bf16[128,4096]{1,0:T(8,128)(2,1)} %v_ref.1, ...), custom_call_target="tpu_custom_call" | custom-call | tf_op jit(solution)/shard_map/front/pallas_call | solution.py:274
  211.5 0.0 copy-done
  211.5 0.0 copy-done.3
  211.5 0.0 copy-done.4
  211.6 0.0 copy-start.1
  211.6 1.2 copy-done.1
  212.8 1.5 route.1
  214.3 39.3 %all_to_all.10 = bf16[8,40,4096]{2,1,0:T(8,128)(2,1)} all-to-all(bf16[8,40,4096]{2,1,0:T(8,128)(2,1)S(1)} %bitcast.11), channel_id=1, replica_groups=mesh['dp'=8,'ctx'=8,'exp'=4] {'ctx'}, dimensions={0} | all-to-all | bytes 5242880 | tf_op jit(solution)/shard_map/all_to_all | solution.py:443
  253.6 17.1 %experts.1 = bf16[320,4096]{1,0:T(8,128)(2,1)} custom-call(bf16[320,4096]{1,0:T(8,128)(2,1)} %bitcast.14, bf16[4096,256]{1,0:T(8,128)(2,1)} %bitcast.17, bf16[4096,256]{1,0:T(8,128)(2,1)} %bitcast.19, bf16[4096,256]{1,0:T(8,128)(2,1)} %bitcast.21, bf16[3,4096,256]{2,1,0:T(8,128)(2,1)} %get-tuple-element.13.gate_ref, ...), custom_call_target="tpu_custom_call" | custom-call | tf_op jit(solution)/shard_map/experts/pallas_call | solution.py:400
  270.7 0.0 copy-start.2
  270.7 36.9 %all_to_all.11 = bf16[8,40,4096]{2,1,0:T(8,128)(2,1)S(1)} all-to-all(bf16[8,40,4096]{2,1,0:T(8,128)(2,1)} %bitcast.15), channel_id=1, replica_groups=mesh['dp'=8,'ctx'=8,'exp'=4] {'ctx'}, dimensions={0} | all-to-all | bytes 5242880 | tf_op jit(solution)/shard_map/all_to_all | solution.py:447
  307.6 0.0 copy-done.2
  307.6 2.8 combine.1
Async XLA Ops:
  0.7 210.8 %copy-start = (bf16[128,4096]{1,0:T(8,128)(2,1)S(1)}, bf16[128,4096]{1,0:T(8,128)(2,1)}, u32[]{:S(2)}) copy-start(bf16[128,4096]{1,0:T(8,128)(2,1)} %res_ref.3) | copy-start | bytes 3145732
  0.7 210.8 %copy-start.3 = (bf16[4096,8]{0,1:T(8,128)(2,1)S(1)}, bf16[4096,8]{0,1:T(8,128)(2,1)}, u32[]{:S(2)}) copy-start(bf16[4096,8]{0,1:T(8,128)(2,1)} %param.16) | copy-start | bytes 196612
  0.7 210.8 %copy-start.4 = (s32[128,2]{0,1:T(2,128)S(1)}, s32[128,2]{0,1:T(2,128)}, u32[]{:S(2)}) copy-start(s32[128,2]{0,1:T(2,128)} %param.20) | copy-start | bytes 3076
  211.6 1.2 copy-start.1
  270.7 36.9 %copy-start.2 = (bf16[32,128,128]{2,1,0:T(8,128)(2,1)S(1)}, bf16[32,128,128]{2,1,0:T(8,128)(2,1)}, u32[]{:S(2)}) copy-start(bf16[32,128,128]{2,1,0:T(8,128)(2,1)} %get-tuple-element.11.heads_ref) | copy-start | bytes 3145732

commit v3 on v2

v3 whole, which is shorter than its diff:
```python
import functools
import math

import jax
import jax.numpy as jnp
from jax import lax
from jax.experimental import pallas as pl
from jax.experimental.pallas import tpu as pltpu
from jax.sharding import PartitionSpec as P

EPSILON = 1e-05
OUT_SCALE = 0.8
LOG2E = math.log2(math.e)
LOW = -1e30
LANES = 128
SLOTS = 40
ROOM = 48
MIB = 1024 * 1024
MESH = pl.DeviceIdType.MESH
contract_last = (((1,), (1,)), ((), ()))
contract_first = (((0,), (0,)), ((), ()))


def relative(ctx=0, exp=0, dp=0):
    def place(axis, step):
        size = lax.axis_size(axis)
        return lax.rem(lax.axis_index(axis) + step + size, size)

    return {"dp": place("dp", dp), "ctx": place("ctx", ctx), "exp": place("exp", exp)}


def attend_columns(res_ref, heads_ref, h):
    columns = slice(h * LANES, (h + 1) * LANES)
    return res_ref[:, columns].astype(jnp.float32) + heads_ref[h].astype(jnp.float32)


PARTS = 8
AHEAD = 4


def front_kernel(
    bq, bk, lam_ref, q_ref, k_ref, v_ref, gate_ref, up_ref, down_ref, res_ref, router_ref, routes_ref, cap_ref,
    heads_ref, gates_ref, x_ref, w_ref,
    qkv, mixed, kk, vv, qq, acc, largest, normed, buf,
    qkv_send, qkv_recv, out_send, out_recv, x_send, x_recv, w_send, far_recv, w_recv,
):
    _, sources, rows, width = qkv.shape
    length = sources * rows
    half = width // 2
    experts = buf.shape[0]
    fan = lax.axis_size("exp")
    me = lax.axis_index("ctx") * fan + lax.axis_index("exp")
    parity = lax.rem(lax.axis_index("dp"), 2)

    def member(index):
        return {"dp": lax.axis_index("dp"), "ctx": lax.div(index, fan), "exp": lax.rem(index, fan)}

    barrier = pltpu.get_barrier_semaphore()

    def greet(step, carried):
        pl.semaphore_signal(
            barrier, inc=1, device_id=member(lax.rem(me + step, sources)), device_id_type=MESH
        )
        return carried

    lax.fori_loop(1, sources, greet, 0)
    pl.semaphore_signal(barrier, inc=1, device_id=relative(dp=1), device_id_type=MESH)
    pl.semaphore_signal(barrier, inc=1, device_id=relative(dp=-1), device_id_type=MESH)
    pl.semaphore_wait(barrier, sources + 1)

    inputs = (q_ref, k_ref, v_ref)

    def send_heads(step, carried):
        target = lax.rem(me + step, sources)
        columns = pl.ds(pl.multiple_of(target * width, width), width)
        for which in range(3):
            pltpu.make_async_remote_copy(
                src_ref=inputs[which].at[:, columns],
                dst_ref=qkv.at[which, me],
                send_sem=qkv_send,
                recv_sem=qkv_recv,
                device_id=member(target),
                device_id_type=MESH,
            ).start()
        return carried

    lax.fori_loop(1, sources, send_heads, 0)
    own = pl.ds(pl.multiple_of(me * width, width), width)
    for which in range(3):
        pltpu.make_async_copy(inputs[which].at[:, own], qkv.at[which, me], qkv_recv).start()

    weights = (gate_ref, up_ref, down_ref)
    size = gate_ref.shape[0] // (2 * PARTS)
    total = len(weights) * PARTS

    def rows_of(part):
        return pl.ds(pl.multiple_of((parity * PARTS + part) * size, size), size)

    def push(src, array, slot, part, recv, device):
        pltpu.make_async_remote_copy(
            src_ref=src,
            dst_ref=w_ref.at[array * 3 + slot, rows_of(part)],
            send_sem=w_send,
            recv_sem=recv,
            device_id=device,
            device_id_type=MESH,
        ).start()

    def near(array, slot, part):
        return w_recv.at[(array * 3 + slot) * PARTS + part]

    def arrived(array, slot, part):
        block = w_ref.at[array * 3 + slot, rows_of(part)]
        pltpu.make_async_copy(block, block, near(array, slot, part)).wait()

    def first(k):
        part = lax.rem(k, PARTS)
        for array in range(len(weights)):

            @pl.when(lax.div(k, PARTS) == array)
            def _():
                for slot, step in ((1, 1), (0, -1)):
                    push(
                        weights[array].at[rows_of(part)], array, slot, part,
                        near(array, slot, part), relative(exp=step),
                    )

    def along(array, slot, part):
        push(
            w_ref.at[array * 3 + slot, rows_of(part)], array, slot, part, far_recv,
            relative(dp=1 - 2 * lax.rem(part, 2)),
        )

    def third(k):
        array, part = lax.div(k, PARTS), lax.rem(k, PARTS)
        arrived(array, 2, part)
        along(array, 2, part)

    def event(k, carried):
        array, part = lax.div(k, PARTS), lax.rem(k, PARTS)

        @pl.when(k + AHEAD < total)
        def _():
            first(k + AHEAD)

        odd = lax.rem(part, 2)
        arrived(array, 0, part)
        arrived(array, 1, part)
        slot = 1 - odd
        push(
            w_ref.at[array * 3 + slot, rows_of(part)], array, 2, part,
            near(array, 2, part), relative(exp=1 - 2 * odd),
        )
        along(array, 0, part)
        along(array, 1, part)

        @pl.when(k >= 1)
        def _():
            third(k - 1)

        return carried

    def begin(k, carried):
        first(k)
        return carried

    lax.fori_loop(0, AHEAD, begin, 0)
    lax.fori_loop(0, 4, event, 0)

    pltpu.make_async_copy(qkv, qkv, qkv_recv).wait()
    keys = qkv[1].reshape(length, width)
    kk[:, :width] = keys
    kk[:, width:] = keys
    vv[:, :width] = qkv[2].reshape(length, width)
    vv[:, width:] = jnp.ones((length, width), vv.dtype)

    per = bq // rows
    lam = lam_ref[me]

    def query_block(i, carried):
        lax.fori_loop(4 + i + lax.div(i, 3), 5 + i + lax.div(i, 2), event, 0)
        q = qkv[0, pl.ds(i * per, per)].reshape(bq, width)
        q = q.astype(jnp.float32) * (LOG2E / math.sqrt(half))
        hi = q.astype(jnp.bfloat16)
        lo = (q - hi.astype(jnp.float32)).astype(jnp.bfloat16)
        lower = lax.broadcasted_iota(jnp.int32, (bq, width), 1) < half
        zero = jnp.zeros((bq, width), jnp.bfloat16)
        qq[:bq, :width] = jnp.where(lower, hi, zero)
        qq[:bq, width:] = jnp.where(lower, lo, zero)
        qq[bq:, :width] = jnp.where(lower, zero, hi)
        qq[bq:, width:] = jnp.where(lower, zero, lo)
        acc[...] = jnp.zeros_like(acc)
        largest[...] = jnp.full_like(largest, LOW)

        def scores(j, masked):
            keys_here = pl.ds(pl.multiple_of(j * bk, bk), bk)
            s = lax.dot_general(
                qq[...], kk[keys_here, :], contract_last, preferred_element_type=jnp.float32
            )
            if masked:
                row = i * bq + lax.broadcasted_iota(jnp.int32, (bq, bk), 0)
                col = j * bk + lax.broadcasted_iota(jnp.int32, (bq, bk), 1)
                allowed = col <= row
                s = jnp.where(jnp.concatenate([allowed, allowed], axis=0), s, LOW)
            return s

        def look(j, masked):
            s = scores(j, masked)
            top = largest[...]
            for c in range(0, bk, width):
                top = jnp.maximum(top, s[:, c : c + width])
            largest[...] = top

        def add(j, masked):
            s = scores(j, masked)
            top = largest[...]
            raised = jnp.concatenate(
                [jnp.exp2(s[:, c : c + width] - top).astype(jnp.bfloat16) for c in range(0, bk, width)],
                axis=1,
            )
            keys_here = pl.ds(pl.multiple_of(j * bk, bk), bk)
            acc[...] += jnp.dot(raised, vv[keys_here, :], preferred_element_type=jnp.float32)

        full = lax.div(i * bq, bk)

        def look_body(j, inner):
            look(j, False)
            return inner

        def add_body(j, inner):
            add(j, False)
            return inner

        lax.fori_loop(0, full, look_body, 0)
        look(full, True)
        largest[...] = jnp.broadcast_to(
            jnp.max(largest[...], axis=1, keepdims=True), largest.shape
        )
        lax.fori_loop(0, full, add_body, 0)
        add(full, True)
        one = acc[:bq, :width] / acc[:bq, width:]
        two = acc[bq:, :width] / acc[bq:, width:]
        blend = one - lam * two
        mean = jnp.mean(blend * blend, axis=1, keepdims=True)
        out = (OUT_SCALE * blend * lax.rsqrt(mean + EPSILON)).astype(mixed.dtype)
        mixed[pl.ds(i * per, per)] = out.reshape(per, rows, width)

        def send_rows(r, inner):
            target = i * per + r

            @pl.when(target != me)
            def _():
                pltpu.make_async_remote_copy(
                    src_ref=mixed.at[target],
                    dst_ref=heads_ref.at[me],
                    send_sem=out_send,
                    recv_sem=out_recv,
                    device_id=member(target),
                    device_id_type=MESH,
                ).start()

            @pl.when(target == me)
            def _():
                pltpu.make_async_copy(mixed.at[target], heads_ref.at[me], out_recv).start()

            return inner

        lax.fori_loop(0, per, send_rows, 0)
        return carried

    blocks = length // bq
    lax.fori_loop(0, blocks, query_block, 0)
    pltpu.make_async_copy(heads_ref, heads_ref, out_recv).wait()
    route(res_ref, heads_ref, router_ref, routes_ref, cap_ref, gates_ref, normed, buf)

    here = lax.axis_index("ctx")

    def send_expert(step, carried):
        target = lax.rem(here + step, experts)
        pltpu.make_async_remote_copy(
            src_ref=buf.at[target],
            dst_ref=x_ref.at[here],
            send_sem=x_send,
            recv_sem=x_recv,
            device_id=relative(ctx=step),
            device_id_type=MESH,
        ).start()
        return carried

    lax.fori_loop(1, experts, send_expert, 0)
    pltpu.make_async_copy(buf.at[here], x_ref.at[here], x_recv).start()

    lax.fori_loop(4 + blocks + lax.div(blocks, 3), total, event, 0)
    third(total - 1)
    others = pl.ds(0, sources - 1)
    for which in range(3):
        pltpu.make_async_copy(qkv.at[which, others], qkv.at[which, others], qkv_send).wait()
    pltpu.make_async_copy(mixed.at[others], mixed.at[others], out_send).wait()
    pltpu.make_async_copy(buf.at[pl.ds(1, experts - 1)], buf.at[pl.ds(1, experts - 1)], x_send).wait()
    pltpu.make_async_copy(x_ref, x_ref, x_recv).wait()
    halves = size * PARTS
    far = w_ref.at[:, pl.ds(pl.multiple_of((1 - parity) * halves, halves), halves)]
    pltpu.make_async_copy(far, far, far_recv).wait()
    pltpu.make_async_copy(w_ref, w_ref, w_send).wait()


def route(res_ref, heads_ref, router_ref, routes_ref, cap_ref, gates_ref, normed, buf):
    heads, tokens, width = heads_ref.shape
    experts, room, _ = buf.shape
    square = jnp.zeros((tokens, width), jnp.float32)
    for h in range(heads):
        block = attend_columns(res_ref, heads_ref, h)
        square = square + block * block
    mean = jnp.sum(square, axis=1, keepdims=True) / (heads * width)
    factor = lax.rsqrt(mean + EPSILON)
    for h in range(heads):
        block = attend_columns(res_ref, heads_ref, h)
        normed[:, h * width : (h + 1) * width] = (block * factor).astype(jnp.bfloat16)
    logits = lax.dot_general(
        router_ref[...], normed[...], contract_last, preferred_element_type=jnp.float32
    )
    sig = 1.0 / (1.0 + jnp.exp(-logits))
    expert_of = lax.broadcasted_iota(jnp.int32, (experts, tokens), 0)
    named = (routes_ref[0:1, :] == expert_of) | (routes_ref[1:2, :] == expert_of)
    picked = jnp.where(named, sig, 0.0)
    gates = picked / jnp.sum(picked, axis=0, keepdims=True)
    before = lax.broadcasted_iota(jnp.int32, (tokens, tokens), 0) < lax.broadcasted_iota(
        jnp.int32, (tokens, tokens), 1
    )
    position = jnp.dot(
        jnp.where(named, 1.0, 0.0).astype(jnp.bfloat16),
        jnp.where(before, 1.0, 0.0).astype(jnp.bfloat16),
        preferred_element_type=jnp.float32,
    )
    kept = named & (position < cap_ref[...].astype(jnp.float32))
    position = jnp.where(kept, position, -1.0).astype(jnp.int32)
    slot = lax.broadcasted_iota(jnp.int32, (room, tokens), 0)
    chosen = [slot == position[e : e + 1, :] for e in range(experts)]
    one_hot = jnp.concatenate([jnp.where(c, 1.0, 0.0) for c in chosen], axis=0).astype(jnp.bfloat16)
    gates_ref[...] = jnp.concatenate(
        [jnp.where(chosen[e][:SLOTS], gates[e : e + 1, :], 0.0) for e in range(experts)], axis=0
    )
    for column in range(0, heads * width, 512):
        columns = slice(column, column + 512)
        moved = jnp.dot(one_hot, normed[:, columns], preferred_element_type=jnp.float32)
        buf[:, :, columns] = moved.astype(jnp.bfloat16).reshape(experts, room, 512)


def front(lambdas, queries, key_rows, value_rows, own, residual, router, routes, capacity, bq=1024, bk=1024):
    rows, total = queries.shape
    experts = router.shape[0]
    width = LANES
    heads = total // width
    length = heads * rows
    anywhere = pl.BlockSpec(memory_space=pl.ANY)
    vmem = pl.BlockSpec(memory_space=pltpu.VMEM)
    slots = len(own) * (lax.axis_size("exp") - 1)
    dma = pltpu.SemaphoreType.DMA
    return pl.pallas_call(
        functools.partial(front_kernel, bq, bk),
        out_shape=(
            jax.ShapeDtypeStruct((heads, rows, width), jnp.bfloat16),
            jax.ShapeDtypeStruct((experts * SLOTS, rows), jnp.float32),
            jax.ShapeDtypeStruct((experts, ROOM, total), jnp.bfloat16),
            jax.ShapeDtypeStruct((slots, *own[0].shape), jnp.bfloat16),
        ),
        in_specs=[pl.BlockSpec(memory_space=pltpu.SMEM)] + [anywhere] * 6 + [vmem] * 4,
        out_specs=(vmem, vmem, anywhere, anywhere),
        scratch_shapes=[
            pltpu.VMEM((3, heads, rows, width), jnp.bfloat16),
            pltpu.VMEM((heads, rows, width), jnp.bfloat16),
            pltpu.VMEM((length, 2 * width), jnp.bfloat16),
            pltpu.VMEM((length, 2 * width), jnp.bfloat16),
            pltpu.VMEM((2 * bq, 2 * width), jnp.bfloat16),
            pltpu.VMEM((2 * bq, 2 * width), jnp.float32),
            pltpu.VMEM((2 * bq, width), jnp.float32),
            pltpu.VMEM((rows, total), jnp.bfloat16),
            pltpu.VMEM((experts, ROOM, total), jnp.bfloat16),
        ]
        + [dma] * 8
        + [dma((slots * PARTS,))],
        compiler_params=pltpu.CompilerParams(
            vmem_limit_bytes=58 * MIB, collective_id=0, has_side_effects=True
        ),
        name="front",
    )(lambdas, queries, key_rows, value_rows, *own, residual, router, routes, capacity)


def expert_kernel(x_ref, gate_own, up_own, down_own, gate_ref, up_ref, down_ref, o_ref, x_all, acc):
    group = pl.program_id(0)
    sources, _, width = x_ref.shape

    def contribute(gate_w, up_w, down_w, begin):
        x = x_all[...]
        gate_out = jnp.dot(x, gate_w[...], preferred_element_type=jnp.float32)
        up_out = jnp.dot(x, up_w[...], preferred_element_type=jnp.float32)
        hidden = (gate_out / (1.0 + jnp.exp(-gate_out)) * up_out).astype(jnp.bfloat16)
        for c in range(0, width, 512):
            part = lax.dot_general(
                hidden, down_w[c : c + 512, :], contract_last, preferred_element_type=jnp.float32
            ).astype(jnp.bfloat16).astype(jnp.float32)
            if begin:
                acc[:, c : c + 512] = part
            else:
                acc[:, c : c + 512] += part

    @pl.when(group == 0)
    def _():
        for c in range(0, width, 512):
            parts = [
                x_ref[s, :, c : c + 512].astype(jnp.float32)[:SLOTS] for s in range(sources)
            ]
            x_all[:, c : c + 512] = jnp.concatenate(parts, axis=0).astype(x_all.dtype)
        contribute(gate_own, up_own, down_own, True)

    @pl.when(group > 0)
    def _():
        contribute(gate_ref, up_ref, down_ref, False)

    @pl.when(group == pl.num_programs(0) - 1)
    def _():
        o_ref[...] = acc[...].astype(o_ref.dtype)


def expert(x, own, others):
    sources, room, width = x.shape
    rows = sources * SLOTS
    slots, _, hidden = others.shape
    arrays = len(own)
    each = slots // arrays
    whole = pl.BlockSpec((width, hidden), lambda g: (0, 0), pipeline_mode=pl.Buffered(1))

    def weight(array):
        return pl.BlockSpec(
            (None, width, hidden), lambda g: (array * each + jnp.maximum(g - 1, 0), 0, 0)
        )

    return pl.pallas_call(
        expert_kernel,
        grid=(each + 1,),
        out_shape=jax.ShapeDtypeStruct((rows, width), jnp.bfloat16),
        in_specs=[pl.BlockSpec((sources, room, width), lambda g: (0, 0, 0), pipeline_mode=pl.Buffered(1))]
        + [whole] * arrays
        + [weight(a) for a in range(arrays)],
        out_specs=pl.BlockSpec((rows, width), lambda g: (0, 0)),
        scratch_shapes=[pltpu.VMEM((rows, width), jnp.bfloat16), pltpu.VMEM((rows, width), jnp.float32)],
        compiler_params=pltpu.CompilerParams(vmem_limit_bytes=56 * MIB),
        name="experts",
    )(x, *own, others, others, others)


def combine_kernel(res_ref, heads_ref, back_ref, gate_ref, o_ref):
    heads = heads_ref.shape[0]
    gates = gate_ref[...]
    hi = gates.astype(jnp.bfloat16)
    lo = (gates - hi.astype(jnp.float32)).astype(jnp.bfloat16)
    for h in range(heads):
        columns = slice(h * LANES, (h + 1) * LANES)
        back = back_ref[:, columns]
        total = lax.dot_general(hi, back, contract_first, preferred_element_type=jnp.float32)
        total += lax.dot_general(lo, back, contract_first, preferred_element_type=jnp.float32)
        o_ref[:, columns] = (attend_columns(res_ref, heads_ref, h) + total).astype(o_ref.dtype)


def combine(residual, heads, back, gates):
    return pl.pallas_call(
        combine_kernel,
        out_shape=jax.ShapeDtypeStruct(residual.shape, jnp.bfloat16),
        compiler_params=pltpu.CompilerParams(vmem_limit_bytes=48 * MIB),
        name="combine",
    )(residual, heads, back, gates)


def shards(
    queries, key_rows, value_rows, residual, lambdas, router, gate_proj, up_proj, down_proj, routes, capacity
):
    tokens, width = queries.shape
    experts = router.shape[1]
    own = (gate_proj[0], up_proj[0], down_proj[0])
    mixed, gates, x, others = front(
        lambdas, queries, key_rows, value_rows, own, residual, router.T, routes.T, capacity.T
    )
    results = expert(x, own, others)
    back = lax.all_to_all(
        results.reshape(experts, SLOTS, width), "ctx", split_axis=0, concat_axis=0, tiled=True
    )
    return combine(residual, mixed, back.reshape(experts * SLOTS, width), gates)


def solution(mesh):
    rows = P(("dp", "ctx", "exp"), None)
    weights = P("ctx", None, "exp")
    placed = (rows, rows, rows, rows, P(), P(), weights, weights, weights, rows, rows)
    return jax.shard_map(shards, mesh=mesh, in_specs=placed, out_specs=rows, check_vma=False)
```

time: 314 us -> 282 us (0.90)
  blocking collectives: 76.2 us -> 57.9 us
  Pallas kernels: 232 us -> 222 us
    all_to_all x1 -> x0, blocking collectives: 39.3 us -> none  [shards(): lax.all_to_all(buffer.reshape(experts, SLOTS, width), 'ctx', split_axis=0...]
    all_to_all x1, blocking collectives: 36.9 us -> 57.9 us  [shards(): lax.all_to_all(results.reshape(experts, SLOTS, width), 'ctx', split_axis=...]
    pallas_call x1, Pallas kernels: 211 us -> 202 us  [front(): pl.pallas_call(functools.partial(front_kernel, bq, bk), out_shape=(jax.Sh...]
    pallas_call x2 -> x1, Pallas kernels: 18.6 us -> 17.5 us  [expert(): pl.pallas_call(expert_kernel, grid=(each + 1,), out_shape=jax.ShapeDtypeS...]
where the time goes in v3:
time: 282 us; the launch traced here: 281 us
  Pallas kernels  222 us (79%)
  blocking collectives  57.9 us (21%)
    pallas_call x1, Pallas kernels, front(): pl.pallas_call(functools.partial(front_kernel, bq, bk), out_shape=(jax.Sh...  202 us
    all_to_all x1, blocking collectives, shards(): lax.all_to_all(results.reshape(experts, SLOTS, width), 'ctx', split_axis=...  57.9 us
    pallas_call x1, Pallas kernels, expert(): pl.pallas_call(expert_kernel, grid=(each + 1,), out_shape=jax.ShapeDtypeS...  17.5 us

profile of v3, /device:TPU:120, one launch (start us, length us, event | category | flops | bytes accessed | tf_op | source)
XLA Modules:
  0.0 281.4 jit_solution(9078600788165556590)
XLA Ops:
  0.0 1.3 copy.12.cap_ref
  1.3 201.9 %front.1 = (bf16[32,128,128]{2,1,0:T(8,128)(2,1)}, f32[320,128]{1,0:T(8,128)}, bf16[8,48,4096]{2,1,0:T(8,128)(2,1)}, bf16[9,4096,256]{2,1,0:T(8,128)(2,1)}) custom-call(f32[32]{0:T(128)} %lam_ref.1, bf16[128,4096]{1,0:T(8,128)(2,1)} %q_ref.1, bf16[128,4096]{1,0:T(8,128)(2,1)} %k_ref.1, bf16[128,4096]{1,0:T(8,128)(2,1)} %v_ref.1, bf16[4096,256]{1,0:T(8,128)(2,1)} %bitcast.10, ...), custom_call_target="tpu_custom_call" | custom-call | tf_op jit(solution)/shard_map/front/pallas_call | solution.py:359
  203.2 17.5 %experts.1 = bf16[320,4096]{1,0:T(8,128)(2,1)} custom-call(bf16[8,48,4096]{2,1,0:T(8,128)(2,1)} %get-tuple-element.10.x_ref, bf16[4096,256]{1,0:T(8,128)(2,1)} %bitcast.11, bf16[4096,256]{1,0:T(8,128)(2,1)} %bitcast.13, bf16[4096,256]{1,0:T(8,128)(2,1)} %bitcast.15, bf16[9,4096,256]{2,1,0:T(8,128)(2,1)} %get-tuple-element.11.gate_ref.up_ref.down_ref, ...), custom_call_target="tpu_custom_call" | custom-call | tf_op jit(solution)/shard_map/experts/pallas_call | solution.py:438
  220.6 0.0 copy-start
  220.7 0.0 copy-start.1
  220.7 0.0 copy-start.2
  220.7 57.9 %all_to_all.5 = bf16[8,40,4096]{2,1,0:T(8,128)(2,1)S(1)} all-to-all(bf16[8,40,4096]{2,1,0:T(8,128)(2,1)} %bitcast.9), channel_id=1, replica_groups=mesh['dp'=8,'ctx'=8,'exp'=4] {'ctx'}, dimensions={0} | all-to-all | bytes 5242880 | tf_op jit(solution)/shard_map/all_to_all | solution.py:484
  278.6 0.0 copy-done
  278.6 0.0 copy-done.1
  278.6 0.0 copy-done.2
  278.6 2.8 %combine.1 = bf16[128,4096]{1,0:T(8,128)(2,1)} custom-call(bf16[128,4096]{1,0:T(8,128)(2,1)S(1)} %copy-done, bf16[32,128,128]{2,1,0:T(8,128)(2,1)S(1)} %copy-done.1, bf16[320,4096]{1,0:T(8,128)(2,1)S(1)} %bitcast.8, f32[320,128]{1,0:T(8,128)S(1)} %copy-done.2), custom_call_target="tpu_custom_call" | custom-call | tf_op jit(solution)/shard_map/combine/pallas_call | solution.py:466
Async XLA Ops:
  220.6 57.9 %copy-start = (bf16[128,4096]{1,0:T(8,128)(2,1)S(1)}, bf16[128,4096]{1,0:T(8,128)(2,1)}, u32[]{:S(2)}) copy-start(bf16[128,4096]{1,0:T(8,128)(2,1)} %res_ref.3) | copy-start | bytes 3145732
  220.7 57.9 %copy-start.1 = (bf16[32,128,128]{2,1,0:T(8,128)(2,1)S(1)}, bf16[32,128,128]{2,1,0:T(8,128)(2,1)}, u32[]{:S(2)}) copy-start(bf16[32,128,128]{2,1,0:T(8,128)(2,1)} %get-tuple-element.9.heads_ref) | copy-start | bytes 3145732
  220.7 57.9 %copy-start.2 = (f32[320,128]{1,0:T(8,128)S(1)}, f32[320,128]{1,0:T(8,128)}, u32[]{:S(2)}) copy-start(f32[320,128]{1,0:T(8,128)} %get-tuple-element.12.gate_ref) | copy-start | bytes 491524

commit v4 on v3

--- a/solution.py
+++ b/solution.py
@@ -35,7 +35,8 @@
 
 
 PARTS = 8
-AHEAD = 4
+EARLY = 3
+AHEAD = 3
 
 
 def front_kernel(
@@ -154,9 +155,9 @@
         along(array, 0, part)
         along(array, 1, part)
 
-        @pl.when(k >= 1)
+        @pl.when(k >= 2)
         def _():
-            third(k - 1)
+            third(k - 2)
 
         return carried
 
@@ -165,7 +166,7 @@
         return carried
 
     lax.fori_loop(0, AHEAD, begin, 0)
-    lax.fori_loop(0, 4, event, 0)
+    lax.fori_loop(0, EARLY, event, 0)
 
     pltpu.make_async_copy(qkv, qkv, qkv_recv).wait()
     keys = qkv[1].reshape(length, width)
@@ -177,8 +178,20 @@
     per = bq // rows
     lam = lam_ref[me]
 
-    def query_block(i, carried):
-        lax.fori_loop(4 + i + lax.div(i, 3), 5 + i + lax.div(i, 2), event, 0)
+    blocks = length // bq
+    start = lax.rem(lax.axis_index("ctx"), blocks)
+    chunks = blocks * (blocks + 1) // 2
+
+    def query_block(turn, carried):
+        i = lax.rem(start + turn, blocks)
+        done = EARLY + chunks * lax.div(start + turn, blocks)
+        done = done + lax.div(i * (i + 1), 2) - lax.div(start * (start + 1), 2)
+
+        def weight_step(j, phase):
+            @pl.when(lax.rem(j, 2) == phase)
+            def _():
+                event(done + lax.div(j, 2) + phase * (lax.div(i, 2) + 1), 0)
+
         q = qkv[0, pl.ds(i * per, per)].reshape(bq, width)
         q = q.astype(jnp.float32) * (LOG2E / math.sqrt(half))
         hi = q.astype(jnp.bfloat16)
@@ -205,6 +218,7 @@
             return s
 
         def look(j, masked):
+            weight_step(j, 0)
             s = scores(j, masked)
             top = largest[...]
             for c in range(0, bk, width):
@@ -212,6 +226,7 @@
             largest[...] = top
 
         def add(j, masked):
+            weight_step(j, 1)
             s = scores(j, masked)
             top = largest[...]
             raised = jnp.concatenate(
@@ -268,7 +283,6 @@
         lax.fori_loop(0, per, send_rows, 0)
         return carried
 
-    blocks = length // bq
     lax.fori_loop(0, blocks, query_block, 0)
     pltpu.make_async_copy(heads_ref, heads_ref, out_recv).wait()
     route(res_ref, heads_ref, router_ref, routes_ref, cap_ref, gates_ref, normed, buf)
@@ -290,7 +304,8 @@
     lax.fori_loop(1, experts, send_expert, 0)
     pltpu.make_async_copy(buf.at[here], x_ref.at[here], x_recv).start()
 
-    lax.fori_loop(4 + blocks + lax.div(blocks, 3), total, event, 0)
+    lax.fori_loop(EARLY + chunks, total, event, 0)
+    third(total - 2)
     third(total - 1)
     others = pl.ds(0, sources - 1)
     for which in range(3):

time: 282 us -> 244 us (0.87)
  Pallas kernels: 222 us -> 200 us
  blocking collectives: 57.9 us -> 40.7 us
    pallas_call x1, Pallas kernels: 202 us -> 180 us  [front(): pl.pallas_call(functools.partial(front_kernel, bq, bk), out_shape=(jax.Sh...]
    all_to_all x1, blocking collectives: 57.9 us -> 40.7 us  [shards(): lax.all_to_all(results.reshape(experts, SLOTS, width), 'ctx', split_axis=...]
where the time goes in v4:
time: 244 us; the launch traced here: 242 us
  Pallas kernels  200 us (82%)
  blocking collectives  40.7 us (17%)
    pallas_call x1, Pallas kernels, front(): pl.pallas_call(functools.partial(front_kernel, bq, bk), out_shape=(jax.Sh...  180 us
    all_to_all x1, blocking collectives, shards(): lax.all_to_all(results.reshape(experts, SLOTS, width), 'ctx', split_axis=...  40.7 us
    pallas_call x1, Pallas kernels, expert(): pl.pallas_call(expert_kernel, grid=(each + 1,), out_shape=jax.ShapeDtypeS...  17.5 us

profile of v4, /device:TPU:120, one launch (start us, length us, event | category | flops | bytes accessed | tf_op | source)
XLA Modules:
  0.0 242.1 jit_solution(7895482268103989927)
XLA Ops:
  0.0 1.3 copy.12.cap_ref
  1.3 179.8 %front.1 = (bf16[32,128,128]{2,1,0:T(8,128)(2,1)}, f32[320,128]{1,0:T(8,128)}, bf16[8,48,4096]{2,1,0:T(8,128)(2,1)}, bf16[9,4096,256]{2,1,0:T(8,128)(2,1)}) custom-call(f32[32]{0:T(128)} %lam_ref.1, bf16[128,4096]{1,0:T(8,128)(2,1)} %q_ref.1, bf16[128,4096]{1,0:T(8,128)(2,1)} %k_ref.1, bf16[128,4096]{1,0:T(8,128)(2,1)} %v_ref.1, bf16[4096,256]{1,0:T(8,128)(2,1)} %bitcast.10, ...), custom_call_target="tpu_custom_call" | custom-call | tf_op jit(solution)/shard_map/front/pallas_call | solution.py:374
  181.1 17.5 %experts.1 = bf16[320,4096]{1,0:T(8,128)(2,1)} custom-call(bf16[8,48,4096]{2,1,0:T(8,128)(2,1)} %get-tuple-element.10.x_ref, bf16[4096,256]{1,0:T(8,128)(2,1)} %bitcast.11, bf16[4096,256]{1,0:T(8,128)(2,1)} %bitcast.13, bf16[4096,256]{1,0:T(8,128)(2,1)} %bitcast.15, bf16[9,4096,256]{2,1,0:T(8,128)(2,1)} %get-tuple-element.11.gate_ref.up_ref.down_ref, ...), custom_call_target="tpu_custom_call" | custom-call | tf_op jit(solution)/shard_map/experts/pallas_call | solution.py:453
  198.6 0.0 copy-start
  198.6 0.0 copy-start.1
  198.6 0.0 copy-start.2
  198.6 40.7 %all_to_all.5 = bf16[8,40,4096]{2,1,0:T(8,128)(2,1)S(1)} all-to-all(bf16[8,40,4096]{2,1,0:T(8,128)(2,1)} %bitcast.9), channel_id=1, replica_groups=mesh['dp'=8,'ctx'=8,'exp'=4] {'ctx'}, dimensions={0} | all-to-all | bytes 5242880 | tf_op jit(solution)/shard_map/all_to_all | solution.py:499
  239.2 0.0 copy-done
  239.2 0.0 copy-done.1
  239.2 0.0 copy-done.2
  239.2 2.8 %combine.1 = bf16[128,4096]{1,0:T(8,128)(2,1)} custom-call(bf16[128,4096]{1,0:T(8,128)(2,1)S(1)} %copy-done, bf16[32,128,128]{2,1,0:T(8,128)(2,1)S(1)} %copy-done.1, bf16[320,4096]{1,0:T(8,128)(2,1)S(1)} %bitcast.8, f32[320,128]{1,0:T(8,128)S(1)} %copy-done.2), custom_call_target="tpu_custom_call" | custom-call | tf_op jit(solution)/shard_map/combine/pallas_call | solution.py:481
Async XLA Ops:
  198.6 40.7 %copy-start = (bf16[128,4096]{1,0:T(8,128)(2,1)S(1)}, bf16[128,4096]{1,0:T(8,128)(2,1)}, u32[]{:S(2)}) copy-start(bf16[128,4096]{1,0:T(8,128)(2,1)} %res_ref.3) | copy-start | bytes 3145732
  198.6 40.7 %copy-start.1 = (bf16[32,128,128]{2,1,0:T(8,128)(2,1)S(1)}, bf16[32,128,128]{2,1,0:T(8,128)(2,1)}, u32[]{:S(2)}) copy-start(bf16[32,128,128]{2,1,0:T(8,128)(2,1)} %get-tuple-element.9.heads_ref) | copy-start | bytes 3145732
  198.6 40.7 %copy-start.2 = (f32[320,128]{1,0:T(8,128)S(1)}, f32[320,128]{1,0:T(8,128)}, u32[]{:S(2)}) copy-start(f32[320,128]{1,0:T(8,128)} %get-tuple-element.12.gate_ref) | copy-start | bytes 491524

commit v5 on v4

--- a/solution.py
+++ b/solution.py
@@ -284,6 +284,7 @@
         return carried
 
     lax.fori_loop(0, blocks, query_block, 0)
+    lax.fori_loop(EARLY + chunks, EARLY + chunks + 2, event, 0)
     pltpu.make_async_copy(heads_ref, heads_ref, out_recv).wait()
     route(res_ref, heads_ref, router_ref, routes_ref, cap_ref, gates_ref, normed, buf)
 
@@ -304,7 +305,7 @@
     lax.fori_loop(1, experts, send_expert, 0)
     pltpu.make_async_copy(buf.at[here], x_ref.at[here], x_recv).start()
 
-    lax.fori_loop(EARLY + chunks, total, event, 0)
+    lax.fori_loop(EARLY + chunks + 2, total, event, 0)
     third(total - 2)
     third(total - 1)
     others = pl.ds(0, sources - 1)

time: 244 us -> 235 us (0.963)
  Pallas kernels: 200 us -> 192 us
    pallas_call x1, Pallas kernels: 180 us -> 171 us  [front(): pl.pallas_call(functools.partial(front_kernel, bq, bk), out_shape=(jax.Sh...]
where the time goes in v5:
time: 235 us; the launch traced here: 234 us
  Pallas kernels  192 us (82%)
  blocking collectives  40.8 us (17%)
    pallas_call x1, Pallas kernels, front(): pl.pallas_call(functools.partial(front_kernel, bq, bk), out_shape=(jax.Sh...  171 us
    all_to_all x1, blocking collectives, shards(): lax.all_to_all(results.reshape(experts, SLOTS, width), 'ctx', split_axis=...  40.8 us
    pallas_call x1, Pallas kernels, expert(): pl.pallas_call(expert_kernel, grid=(each + 1,), out_shape=jax.ShapeDtypeS...  17.5 us

profile of v5, /device:TPU:120, one launch (start us, length us, event | category | flops | bytes accessed | tf_op | source)
XLA Modules:
  0.0 233.7 jit_solution(13515099272664618017)
XLA Ops:
  0.0 1.3 copy.12.cap_ref
  1.3 171.2 %front.1 = (bf16[32,128,128]{2,1,0:T(8,128)(2,1)}, f32[320,128]{1,0:T(8,128)}, bf16[8,48,4096]{2,1,0:T(8,128)(2,1)}, bf16[9,4096,256]{2,1,0:T(8,128)(2,1)}) custom-call(f32[32]{0:T(128)} %lam_ref.1, bf16[128,4096]{1,0:T(8,128)(2,1)} %q_ref.1, bf16[128,4096]{1,0:T(8,128)(2,1)} %k_ref.1, bf16[128,4096]{1,0:T(8,128)(2,1)} %v_ref.1, bf16[4096,256]{1,0:T(8,128)(2,1)} %bitcast.10, ...), custom_call_target="tpu_custom_call" | custom-call | tf_op jit(solution)/shard_map/front/pallas_call | solution.py:375
  172.6 17.5 %experts.1 = bf16[320,4096]{1,0:T(8,128)(2,1)} custom-call(bf16[8,48,4096]{2,1,0:T(8,128)(2,1)} %get-tuple-element.10.x_ref, bf16[4096,256]{1,0:T(8,128)(2,1)} %bitcast.11, bf16[4096,256]{1,0:T(8,128)(2,1)} %bitcast.13, bf16[4096,256]{1,0:T(8,128)(2,1)} %bitcast.15, bf16[9,4096,256]{2,1,0:T(8,128)(2,1)} %get-tuple-element.11.gate_ref.up_ref.down_ref, ...), custom_call_target="tpu_custom_call" | custom-call | tf_op jit(solution)/shard_map/experts/pallas_call | solution.py:454
  190.0 0.0 copy-start
  190.0 0.0 copy-start.1
  190.0 0.0 copy-start.2
  190.0 40.8 %all_to_all.5 = bf16[8,40,4096]{2,1,0:T(8,128)(2,1)S(1)} all-to-all(bf16[8,40,4096]{2,1,0:T(8,128)(2,1)} %bitcast.9), channel_id=1, replica_groups=mesh['dp'=8,'ctx'=8,'exp'=4] {'ctx'}, dimensions={0} | all-to-all | bytes 5242880 | tf_op jit(solution)/shard_map/all_to_all | solution.py:500
  230.9 0.0 copy-done
  230.9 0.0 copy-done.1
  230.9 0.0 copy-done.2
  230.9 2.8 %combine.1 = bf16[128,4096]{1,0:T(8,128)(2,1)} custom-call(bf16[128,4096]{1,0:T(8,128)(2,1)S(1)} %copy-done, bf16[32,128,128]{2,1,0:T(8,128)(2,1)S(1)} %copy-done.1, bf16[320,4096]{1,0:T(8,128)(2,1)S(1)} %bitcast.8, f32[320,128]{1,0:T(8,128)S(1)} %copy-done.2), custom_call_target="tpu_custom_call" | custom-call | tf_op jit(solution)/shard_map/combine/pallas_call | solution.py:482
Async XLA Ops:
  190.0 40.8 %copy-start = (bf16[128,4096]{1,0:T(8,128)(2,1)S(1)}, bf16[128,4096]{1,0:T(8,128)(2,1)}, u32[]{:S(2)}) copy-start(bf16[128,4096]{1,0:T(8,128)(2,1)} %res_ref.3) | copy-start | bytes 3145732
  190.0 40.8 %copy-start.1 = (bf16[32,128,128]{2,1,0:T(8,128)(2,1)S(1)}, bf16[32,128,128]{2,1,0:T(8,128)(2,1)}, u32[]{:S(2)}) copy-start(bf16[32,128,128]{2,1,0:T(8,128)(2,1)} %get-tuple-element.9.heads_ref) | copy-start | bytes 3145732
  190.0 40.8 %copy-start.2 = (f32[320,128]{1,0:T(8,128)S(1)}, f32[320,128]{1,0:T(8,128)}, u32[]{:S(2)}) copy-start(f32[320,128]{1,0:T(8,128)} %get-tuple-element.12.gate_ref) | copy-start | bytes 491524
